TPU v7x, 512 devices: a whole 4x4x16 slice. The times are simulated.
512 devices in a mesh: dp: 16 (over z), seq: 32 (over y, x, core).
Axes of the slice: x: 4, y: 4, z: 16, core: 2. Of those that a mesh axis runs over, the one named last changes fastest.
Arguments:
- queries: bfloat16 [16, 4096, 2048], P('dp', 'seq'), may hold values from -6 to 6
- keys: bfloat16 [16, 4096, 2048], P('dp', 'seq'), may hold values from -6 to 6
- values: bfloat16 [16, 4096, 2048], P('dp', 'seq'), may hold values from -6 to 6
- residual_in: bfloat16 [16, 4096, 2048], P('dp', 'seq'), may hold values from -6 to 6
- cotangent: bfloat16 [16, 4096, 2048], P('dp', 'seq'), may hold values from -0.09375 to 0.09375
- expert_ids: int32 [16, 4096, 2], P('dp', 'seq'), may hold values from 0 to 31, all different within a row; in each aligned block of 128 rows (0 to 127, 128 to 255, ..., all dimensions but the last counted through in order) at most 12 rows name the same one
- router: bfloat16 [2048, 32], replicated, may hold values from -0.125 to 0.125
- attn_gain: float32 [2048], replicated, may hold values from 0.25 to 1.75
- moe_gain: float32 [2048], replicated, may hold values from 0.25 to 1.75
- w_gate: bfloat16 [32, 2048, 256], P('seq', 'dp'), may hold values from -0.125 to 0.125
- w_up: bfloat16 [32, 2048, 256], P('seq', 'dp'), may hold values from -0.125 to 0.125
- w_down: bfloat16 [32, 2048, 256], P('seq', 'dp'), may hold values from -0.375 to 0.375
- trainable: int32 [32], P('seq'), may hold values 0 or 1
Outputs:
- mixed: bfloat16 [16, 4096, 2048], P('dp', 'seq')
- grad_gate: float32 [32, 2048, 256], P('seq', 'dp')
- grad_up: float32 [32, 2048, 256], P('seq', 'dp')
- grad_down: float32 [32, 2048, 256], P('seq', 'dp')
Inputs may be any that keep to these rules, and one draw needn't show every extreme that they name: `expert_ids`: each position names two different experts; among the 128 positions of one index of seq no expert is named by more than 12 choices, a bound that some block reaches.
All inputs are finite; a program needn't handle non-finite values. No bound on the sum of `trainable` on one device may be relied on, other than what follows from the above.
Results may differ from a plain program's by a relative error of at most 0.025.
Values may be sent and summed in bfloat16 or wider, within the bound.
A program may use at most 128 MiB of HBM per device.

v0:
```python
import jax
import jax.numpy as jnp
from jax import lax
from jax.sharding import Mesh
from jax.sharding import PartitionSpec as P

HD = 128
SEQ = ("seq_0", "seq_1", "seq_2")


def nothing_yet(x, identity):
    return jnp.zeros_like(x) + jnp.asarray(identity, x.dtype)


def carried_in(x, axes, combine, identity):
    before = start = nothing_yet(x, identity)
    subtotal = x
    for axis in reversed(axes):
        peers, index = (lax.axis_size(axis), lax.axis_index(axis))
        pieces = lax.all_gather(subtotal.astype(jnp.bfloat16), axis)
        inside, subtotal = (start, start)
        for k in range(peers):
            passed = k < index
            subtotal = combine(subtotal, pieces[k].astype(x.dtype))
            inside = jnp.where(passed, subtotal, inside)
        before = combine(inside, before)
    return before


def in_one_piece(arrays, axis, split_dim, concat_dim, along):
    ends, at = ([], 0)
    for a in arrays[:-1]:
        at += a.shape[along]
        ends.append(at)
    both = jnp.concatenate(arrays, axis=along)
    return tuple(
        jnp.split(
            lax.all_to_all(both, axis, split_axis=split_dim, concat_axis=concat_dim, tiled=True),
            ends,
            axis=along,
        )
    )


def side_by_side(arrays, axis, dim, along):
    widths = [a.shape[along] for a in arrays]
    both = jnp.concatenate(arrays, axis=along)
    filled = lax.all_gather(both, axis, axis=dim, tiled=True)
    return tuple(jnp.split(filled, [sum(widths[:k]) for k in range(1, len(widths))], axis=along))


def side_by_side_2(arrays, axis, dim, along):
    ends, at = ([], 0)
    for a in arrays[:-1]:
        at += a.shape[along]
        ends.append(at)
    both = jnp.concatenate(arrays, axis=along)
    return tuple(
        jnp.split(lax.psum_scatter(both, axis, scatter_dimension=dim, tiled=True), ends, axis=along)
    )


def add_states(earlier, later):
    return earlier + later


def body(
    queries,
    keys,
    values,
    residual_in,
    cotangent,
    expert_ids,
    router,
    attn_gain,
    moe_gain,
    w_gate,
    w_up,
    w_down,
    trainable,
):
    tokens = queries.shape[1]
    width = queries.shape[2]
    heads = width // HD
    experts = router.shape[1]
    peers = lax.axis_size(SEQ)
    slots = max(2, 3 * tokens // peers)
    q_heads = queries[0].reshape(tokens, heads, HD)
    k_heads = keys[0].reshape(tokens, heads, HD)
    v_heads = values[0].reshape(tokens, heads, HD)
    local = jnp.einsum("thd,the->hde", k_heads, v_heads, preferred_element_type=jnp.float32)
    prefix = carried_in(local, SEQ, add_states, jnp.zeros_like(local))
    scores = jnp.einsum("thd,shd->hts", q_heads, k_heads, preferred_element_type=jnp.float32)
    causal = jnp.tril(jnp.ones((tokens, tokens), dtype=bool))
    weights = jnp.where(causal, scores, 0.0).astype(jnp.bfloat16)
    intra = jnp.einsum("hts,shd->thd", weights, v_heads, preferred_element_type=jnp.float32)
    carried = jnp.einsum(
        "thd,hde->the", q_heads.astype(jnp.float32), prefix, precision=lax.Precision.HIGHEST
    )
    attended = intra + carried
    attended = attended * lax.rsqrt(jnp.mean(attended * attended, axis=-1, keepdims=True) + 1e-06)
    stream = residual_in[0].astype(jnp.float32) + attended.reshape(tokens, width) * attn_gain
    normed = (
        stream * lax.rsqrt(jnp.mean(stream * stream, axis=-1, keepdims=True) + 1e-06) * moe_gain
    ).astype(jnp.bfloat16)
    choices_ids = expert_ids[0]
    logits = jnp.dot(normed, router, preferred_element_type=jnp.float32)
    onehot = (choices_ids[..., None] == jnp.arange(experts, dtype=jnp.int32)).astype(jnp.int32)
    chosen = jnp.sum(onehot.astype(jnp.float32) * logits[:, None, :], axis=-1)
    sig = jax.nn.sigmoid(chosen)
    gates = sig / jnp.sum(sig, axis=-1, keepdims=True)
    flat = onehot.reshape(2 * tokens, experts)
    before = jnp.cumsum(flat, axis=0) - flat
    rank = jnp.sum(before * flat, axis=-1)
    target = choices_ids.reshape(2 * tokens) * slots + rank
    placing = (target[:, None] == jnp.arange(experts * slots, dtype=jnp.int32)[None, :]).astype(
        jnp.bfloat16
    )
    contract = (((0,), (0,)), ((), ()))
    both_places = jnp.sum(placing.reshape(tokens, 2, experts * slots), axis=1)
    send_rows = (
        lax.dot_general(both_places, normed, contract, preferred_element_type=jnp.float32)
        .astype(jnp.bfloat16)
        .reshape(experts, slots, width)
    )
    expert_cot = (
        (cotangent[0].astype(jnp.float32)[:, None, :] * gates[:, :, None])
        .reshape(2 * tokens, width)
        .astype(jnp.bfloat16)
    )
    got_rows, got_cot = in_one_piece(
        (
            send_rows,
            lax.dot_general(placing, expert_cot, contract, preferred_element_type=jnp.float32)
            .astype(jnp.bfloat16)
            .reshape(experts, slots, width),
        ),
        SEQ,
        0,
        0,
        1,
    )
    rows = got_rows.reshape(peers * slots, width)
    gate_full, up_full, down_full = side_by_side((w_gate, w_up, w_down), "dp", 1, 0)
    pre_gate = jnp.dot(rows, gate_full[0], preferred_element_type=jnp.float32)
    pre_up = jnp.dot(rows, up_full[0], preferred_element_type=jnp.float32)
    down_mat = down_full[0]
    sigma = jax.nn.sigmoid(pre_gate)
    act = pre_gate * sigma
    hidden = (act * pre_up).astype(jnp.bfloat16)
    expert_out = lax.dot_general(
        hidden, down_mat, (((1,), (1,)), ((), ())), preferred_element_type=jnp.float32
    ).astype(jnp.bfloat16)
    back = lax.all_to_all(
        expert_out.reshape(peers, slots, width), SEQ, split_axis=0, concat_axis=0, tiled=True
    )
    gathered = jnp.dot(
        placing, back.reshape(experts * slots, width), preferred_element_type=jnp.float32
    ).reshape(tokens, 2, width)
    mixed = (stream + jnp.sum(gates[:, :, None] * gathered, axis=1)).astype(jnp.bfloat16)
    cot_rows = got_cot.reshape(peers * slots, width)
    flag = trainable[0] > 0
    d_hidden = jnp.dot(cot_rows, down_mat, preferred_element_type=jnp.float32)
    d_gate = (d_hidden * pre_up * sigma * (1.0 + pre_gate * (1.0 - sigma))).astype(jnp.bfloat16)
    d_up = (d_hidden * act).astype(jnp.bfloat16)
    term_gate = lax.dot_general(rows, d_gate, contract, preferred_element_type=jnp.float32)
    term_up = lax.dot_general(rows, d_up, contract, preferred_element_type=jnp.float32)
    term_down = lax.dot_general(cot_rows, hidden, contract, preferred_element_type=jnp.float32)
    terms = (term_gate, term_up, term_down)
    summed = tuple(
        (
            part.astype(jnp.float32)
            for part in side_by_side_2(
                (
                    terms[0][None].astype(jnp.bfloat16),
                    terms[1][None].astype(jnp.bfloat16),
                    terms[2][None].astype(jnp.bfloat16),
                ),
                "dp",
                1,
                0,
            )
        )
    )
    scale = flag.astype(jnp.float32)
    return (mixed[None], summed[0] * scale, summed[1] * scale, summed[2] * scale)


def solution(mesh):
    finer = Mesh(mesh.devices.reshape(mesh.shape["dp"], 4, 4, 2), ("dp", "seq_0", "seq_1", "seq_2"))
    placed = (
        P("dp", SEQ, None),
        P("dp", SEQ, None),
        P("dp", SEQ, None),
        P("dp", SEQ, None),
        P("dp", SEQ, None),
        P("dp", SEQ, None),
        P(),
        P(),
        P(),
        P(SEQ, "dp", None),
        P(SEQ, "dp", None),
        P(SEQ, "dp", None),
        P(SEQ),
    )
    return jax.shard_map(
        body,
        mesh=finer,
        in_specs=placed,
        out_specs=(P("dp", SEQ, None), P(SEQ, "dp", None), P(SEQ, "dp", None), P(SEQ, "dp", None)),
        check_vma=False,
    )
```

profile of v0, /device:TPU:4, one launch (start us, length us, event | category | flops | bytes accessed | tf_op | source)
XLA Modules:
  0.0 290.3 jit_solution(12224932929899078522)
XLA Ops:
  7.2 1.3 copy.75
  10.9 24.0 %all-gather.12.cloned.1.call-done = bf16[32,128,128]{2,1,0:T(8,128)(2,1)} async-done(((bf16[16,128,128]{2,1,0:T(8,128)(2,1)}), bf16[32,128,128]{2,1,0:T(8,128)(2,1)}) %all-gather.12.cloned.1.call-update) | async-done | bytes 1048592 | tf_op jit(solution)/shard_map/all_gather | solution.py:20
  34.9 2.1 fusion.34
  37.2 39.1 %all-gather.6.cloned.1.call-done = bf16[4,16,128,128]{3,2,1,0:T(8,128)(2,1)} async-done(((bf16[1,16,128,128]{3,2,1,0:T(8,128)(2,1)}), bf16[4,16,128,128]{3,2,1,0:T(8,128)(2,1)}) %all-gather.6.cloned.1.call-update) | async-done | bytes 2097168 | tf_op jit(solution)/shard_map/all_gather | solution.py:20
  76.2 2.7 fusion.32
  83.8 2.5 mul.155
  86.3 32.7 %all-gather.8.cloned.1.call-done = bf16[4,16,128,128]{3,2,1,0:T(8,128)(2,1)} async-done(((bf16[1,16,128,128]{3,2,1,0:T(8,128)(2,1)}), bf16[4,16,128,128]{3,2,1,0:T(8,128)(2,1)}) %all-gather.8.cloned.1.call-update) | async-done | bytes 2097168 | tf_op jit(solution)/shard_map/all_gather | solution.py:20
  119.0 5.6 %convolution_bitcast_fusion.1 = f32[128,16,128]{0,2,1:T(8,128)} fusion(bf16[4,16,128,128]{3,2,1,0:T(8,128)(2,1)} %all-gather.8.cloned.1.call-done, pred[]{:T(512)S(6)} %gt.42, pred[]{:T(512)S(6)} %gt.43, pred[]{:T(512)S(6)} %gt.38, pred[]{:T(512)S(6)} %gt.34, pred[]{:T(512)S(6)} %gt.41, pred[]{:T(512)S(6)} %gt.40, pred[]{:T(512)S(6)} %gt.39, pred[]{:T(512)S(6)} %gt.37, ...), kind=kOutput, calls=%fused_computation.17 | convolution fusion | flops 410255360 | bytes 6815754 | tf_op jit(solution)/shard_map/thd,hde->the/dot_general | solution.py:97
  124.5 1.9 multiply_reduce_fusion.1
  128.8 1.8 convolution_convert_fusion.2
  130.6 2.4 reshape.233
  134.6 3.5 %convolution_convert_fusion.1 = bf16[384,2048]{1,0:T(8,128)(2,1)} fusion(f32[256,2048]{1,0:T(8,128)} %mul.155, f32[256]{0:T(256)S(1)} %reshape.247, s32[256]{0:T(256)S(1)} %multiply_add_fusion.1), kind=kOutput, calls=%fused_computation.3 | convolution fusion | flops 404586496 | bytes 3672064 | tf_op jit(solution)/shard_map/dot_general | solution.py:134
  138.2 3.6 %reshape.235 = bf16[32,12,2048]{2,1,0:T(8,128)(2,1)} reshape(bf16[384,2048]{1,0:T(8,128)(2,1)} %convolution_convert_fusion.1) | data formatting | bytes 3145728 | tf_op jit(solution)/shard_map/reshape | solution.py:136
  141.8 2.5 pad_maximum_fusion
  144.3 43.7 %all_to_all.10 = bf16[32,24,2048]{2,1,0:T(8,128)(2,1)S(1)} all-to-all(bf16[32,24,2048]{2,1,0:T(8,128)(2,1)S(1)} %pad_maximum_fusion), channel_id=1, replica_groups=mesh['dp'=16,'seq_0'=4,'seq_1'=4,'seq_2'=2] {'seq_0','seq_1','seq_2'}, dimensions={0} | all-to-all | bytes 6291456 | tf_op jit(solution)/shard_map/all_to_all | solution.py:38
  188.0 2.3 fusion.81
  190.2 3.6 %reshape.236 = bf16[384,2048]{1,0:T(8,128)(2,1)} reshape(bf16[32,12,2048]{2,1,0:T(8,128)(2,1)} %get-tuple-element.5) | data formatting | bytes 3145728 | tf_op jit(solution)/shard_map/reshape | solution.py:143
  193.9 1.3 reshape.239
  195.2 2.0 all-gather.10.cloned.1.call-done
  197.2 2.3 fusion.24
  199.5 1.9 fusion.33
  202.2 1.8 multiply_convert_fusion.5
  205.7 2.0 pad_maximum_fusion.1
  207.7 1.8 convolution_convert_fusion
  209.5 1.5 reshape.237
  211.1 7.4 %all-to-all-start.1 = ((bf16[32,12,2048]{2,1,0:T(8,128)(2,1)}), bf16[32,12,2048]{2,1,0:T(8,128)(2,1)S(1)}, u32[]{:S(2)}, u32[]{:S(2)}) async-start(bf16[32,12,2048]{2,1,0:T(8,128)(2,1)} %reshape.237), calls=%async_computation.1 | async-start | bytes 4194304 | tf_op jit(solution)/shard_map/all_to_all | solution.py:154
  219.1 1.3 copy.64
  220.4 24.6 %all-to-all-done.1 = bf16[32,12,2048]{2,1,0:T(8,128)(2,1)S(1)} async-done(((bf16[32,12,2048]{2,1,0:T(8,128)(2,1)}), bf16[32,12,2048]{2,1,0:T(8,128)(2,1)S(1)}, u32[]{:S(2)}, u32[]{:S(2)}) %all-to-all-start.1) | async-done | bytes 1572896 | tf_op jit(solution)/shard_map/all_to_all | solution.py:154
  245.0 1.3 reshape.263
  246.4 2.4 fusion.3
  249.8 32.3 %reduce-scatter.2.cloned.1.call-done = bf16[3,128,256]{2,1,0:T(8,128)(2,1)} async-done(((bf16[3,2048,256]{2,1,0:T(8,128)(2,1)}), bf16[3,128,256]{2,1,0:T(8,128)(2,1)}) %reduce-scatter.2.cloned.1.call-update) | async-done | bytes 196624 | tf_op jit(solution)/shard_map/reduce_scatter | solution.py:59
  282.1 1.7 convert_multiply_fusion
  (80 shorter events, 14.6 us)
Async XLA Ops:
  7.2 125.8 %copy-start = (bf16[2048,32]{0,1:T(8,128)(2,1)S(1)}, bf16[2048,32]{0,1:T(8,128)(2,1)}, u32[]{:S(2)}) copy-start(bf16[2048,32]{0,1:T(8,128)(2,1)} %param.19) | copy-start | bytes 393220
  7.2 27.7 %all-gather.12.cloned.1.call-start = ((), (), s32[]{:S(2)}) async-start(), calls=%async_computation.7 | async-start | bytes 1572864 | tf_op jit(solution)/shard_map/all_gather | solution.py:20
  10.8 65.4 %all-gather.6.cloned.1.call-start = ((), (), s32[]{:S(2)}) async-start(), calls=%async_computation.3 | async-start | bytes 2621440 | tf_op jit(solution)/shard_map/all_gather | solution.py:20
  37.1 41.9 %copy-start.11 = (bf16[1,128,256]{2,1,0:T(8,128)(2,1)S(1)}, bf16[1,128,256]{2,1,0:T(8,128)(2,1)}, u32[]{:S(2)}) copy-start(bf16[1,128,256]{2,1,0:T(8,128)(2,1)} %param.24) | copy-start | bytes 196612
  37.1 41.9 %copy-start.12 = (bf16[1,128,256]{2,1,0:T(8,128)(2,1)S(1)}, bf16[1,128,256]{2,1,0:T(8,128)(2,1)}, u32[]{:S(2)}) copy-start(bf16[1,128,256]{2,1,0:T(8,128)(2,1)} %param.23) | copy-start | bytes 196612
  37.1 41.9 %copy-start.13 = (bf16[1,128,256]{2,1,0:T(8,128)(2,1)S(1)}, bf16[1,128,256]{2,1,0:T(8,128)(2,1)}, u32[]{:S(2)}) copy-start(bf16[1,128,256]{2,1,0:T(8,128)(2,1)} %param.22) | copy-start | bytes 196612
  37.1 42.8 %copy-start.15 = (s32[1,128,2]{1,2,0:T(2,128)S(1)}, s32[1,128,2]{1,2,0:T(2,128)}, u32[]{:S(2)}) copy-start(s32[1,128,2]{1,2,0:T(2,128)} %param.18) | copy-start | bytes 3076
  37.1 44.2 %copy-start.9 = (bf16[1,128,2048]{2,1,0:T(8,128)(2,1)S(1)}, bf16[1,128,2048]{2,1,0:T(8,128)(2,1)}, u32[]{:S(2)}) copy-start(bf16[1,128,2048]{2,1,0:T(8,128)(2,1)} %param.13) | copy-start | bytes 1572868
  37.1 81.9 %all-gather.8.cloned.1.call-start = ((), (), s32[]{:S(2)}) async-start(), calls=%async_computation.4 | async-start | bytes 2621440 | tf_op jit(solution)/shard_map/all_gather | solution.py:20
  78.9 3.6 %copy-start.8 = (bf16[1,128,2048]{2,1,0:T(8,128)(2,1)S(1)}, bf16[1,128,2048]{2,1,0:T(8,128)(2,1)}, u32[]{:S(2)}) copy-start(bf16[1,128,2048]{2,1,0:T(8,128)(2,1)} %param.17) | copy-start | bytes 1572868
  78.9 118.2 %all-gather.10.cloned.1.call-start = ((), (), s32[]{:S(2)}) async-start(), calls=%async_computation.5 | async-start | bytes 3342336 | tf_op jit(solution)/shard_map/all_gather | solution.py:48
  79.7 202.4 %reduce-scatter.2.cloned.1.call-start = ((), (), s32[]{:S(2)}) async-start(), calls=%async_computation.6 | async-start | bytes 3342336 | tf_op jit(solution)/shard_map/reduce_scatter | solution.py:59
  119.0 5.6 %copy-start.5 = (bf16[16,8,16,128]{3,2,1,0:T(8,128)(2,1)S(1)}, bf16[16,8,16,128]{3,2,1,0:T(8,128)(2,1)}, u32[]{:S(2)}) copy-start(bf16[16,8,16,128]{3,2,1,0:T(8,128)(2,1)} %copy.77) | copy-start | bytes 1572868
  126.4 1.0 copy-start.1
  126.4 1.0 copy-start.10
  126.6 1.2 copy-start.14
  128.0 0.8 copy-start.3
  195.2 4.2 %copy-start.6 = (bf16[384,2048]{1,0:T(8,128)(2,1)S(1)}, bf16[384,2048]{1,0:T(8,128)(2,1)}, u32[]{:S(2)}) copy-start(bf16[384,2048]{1,0:T(8,128)(2,1)} %reshape.239) | copy-start | bytes 4718596
  199.5 1.9 copy-start.7
  211.1 33.9 %all-to-all-start.1 = ((bf16[32,12,2048]{2,1,0:T(8,128)(2,1)}), bf16[32,12,2048]{2,1,0:T(8,128)(2,1)S(1)}, u32[]{:S(2)}, u32[]{:S(2)}) async-start(bf16[32,12,2048]{2,1,0:T(8,128)(2,1)} %reshape.237), calls=%async_computation.1 | async-start | bytes 4194304 | tf_op jit(solution)/shard_map/all_to_all | solution.py:154
  246.3 2.5 copy-start.2
  246.4 2.5 copy-start.4
Sparse Core Ops, SparseCore 0:
  11.0 23.9 all-gather.11
  37.6 38.5 all-gather.5
  79.1 39.8 all-gather.7
  120.9 76.2 all-gather.9
  207.8 74.2 reduce-scatter.1
where the time goes:
time: 291 us; the launch traced here: 290 us
  waiting for transfers between devices  155 us (53%)
  blocking collectives  43.7 us (15%)
  matrix products  27.9 us (10%)
  local copies, waits for them, and re-layouts  27.3 us (9%)
  between operations  14.8 us (5%)
  other arithmetic  14.3 us (5%)
  starting transfers between devices  7.6 us (3%)
    all_gather x3, waiting for transfers between devices, carried_in(): pieces = lax.all_gather(subtotal.astype(jnp.bfloat16), axis)  95.8 us
    all_to_all x1, blocking collectives, in_one_piece(): lax.all_to_all(both, axis, split_axis=split_dim, concat_axis=concat_dim,...  43.7 us
    reduce_scatter x1, waiting for transfers between devices, side_by_side_2(): lax.psum_scatter(both, axis, scatter_dimension=dim, tiled=True)  32.3 us
    all_to_all x1, waiting for transfers between devices, body(): lax.all_to_all(expert_out.reshape(peers, slots, width), SEQ, split_axis=0...  24.6 us
    all_to_all x1, starting transfers between devices, body(): lax.all_to_all(expert_out.reshape(peers, slots, width), SEQ, split_axis=0...  7.39 us
  transfers between devices with their start and end apart: 6, of which 6 were waited for; matrix products, arithmetic and copies ran while one was open for 16% of the time, Pallas kernels for 0%

commit v1 on v0

v1 whole, which is shorter than its diff:
```python
import functools

import jax
import jax.numpy as jnp
from jax import lax
from jax.experimental import pallas as pl
from jax.experimental.pallas import tpu as pltpu
from jax.sharding import PartitionSpec as P

HD = 128
EPS = 1e-06
MESH = pl.DeviceIdType.MESH
F32 = jnp.float32
BF16 = jnp.bfloat16
Q = 4
GR = 4
SUB = 2


def dot(a, b, ca=1, cb=0):
    return lax.dot_general(a, b, (((ca,), (cb,)), ((), ())), preferred_element_type=F32)


def kernel(
    grid3,
    slots,
    q_ref,
    k_ref,
    v_ref,
    res_ref,
    cot_ref,
    ids_ref,
    router_ref,
    again_ref,
    mgain_ref,
    wg_ref,
    wu_ref,
    wd_ref,
    train_ref,
    mixed_ref,
    gg_ref,
    gu_ref,
    gd_ref,
    w_all,
    st_send,
    st_recv,
    pf_send,
    pf_recv,
    wq,
    stream,
    nst,
    place,
    placeg,
    c_send,
    c_recv,
    x_send,
    x_recv,
    g_send,
    g_recv,
    xs,
    cs,
    pre,
    gcol,
    dgu,
    hid,
    hidg,
    r_send,
    r_recv,
    rs_send,
    rs_recv,
    ag_ss,
    ag_rs,
    p_sem,
    c_ss,
    c_rs,
    x_ss,
    x_rs,
    g_sem,
    r_ss,
    r_rs,
    rr_ss,
    rr_rs,
):
    ny, nx, nc = grid3
    ns = ny * nx * nc
    T, D = q_ref.shape[1], q_ref.shape[2]
    H = D // HD
    DQ = D // Q
    FF = wg_ref.shape[2]
    nz = w_all.shape[0]
    rows_z = w_all.shape[1]
    PR = st_send.shape[1]
    RB = Q * slots
    groups = ns // GR
    GB = GR * RB
    GX = GR * slots
    n_exp = router_ref.shape[0]

    mz = lax.axis_index("dp")
    ms = lax.axis_index("seq")
    mc = ms % nc
    mx = (ms // nc) % nx
    my = ms // (nc * nx)
    right, left = (mz + 1) % nz, (mz + nz - 1) % nz

    def shifted(k, sign):
        dc, dx, dy = k % nc, (k // nc) % nx, k // (nc * nx)
        c = (mc + sign * dc + nc) % nc
        x = (mx + sign * dx + nx) % nx
        y = (my + sign * dy + ny) % ny
        return (y * nx + x) * nc + c

    barrier = pltpu.get_barrier_semaphore()

    def greet(k, carry):
        pl.semaphore_signal(barrier, inc=1, device_id={"seq": shifted(k, 1)}, device_id_type=MESH)
        return carry

    lax.fori_loop(1, ns, greet, 0)
    for z in (left, right):
        pl.semaphore_signal(barrier, inc=1, device_id={"dp": z}, device_id_type=MESH)

    w_all[mz, :, 0:FF] = wg_ref[0]
    w_all[mz, :, FF : 2 * FF] = wu_ref[0]
    w_all[mz, :, 2 * FF : 3 * FF] = wd_ref[0]

    for h in range(H):
        sl = slice(h * HD, (h + 1) * HD)
        state = dot(k_ref[0, :, sl], v_ref[0, :, sl], 0, 0).astype(BF16)
        n = HD // PR
        st_send[h * n : (h + 1) * n] = state.reshape(n, PR, HD)

    pl.semaphore_wait(barrier, ns - 1 + 2)

    n_right, n_left = nz // 2, nz - 1 - nz // 2
    piece = rows_z // SUB

    def ag_copy(way, s, u):
        chunk = (mz + nz - s) % nz if way == 0 else (mz + s) % nz
        ref = w_all.at[chunk, pl.ds(u * piece, piece), :]
        return pltpu.make_async_remote_copy(
            src_ref=ref,
            dst_ref=ref,
            send_sem=ag_ss.at[way, s, u],
            recv_sem=ag_rs.at[way, s, u],
            device_id={"dp": right if way == 0 else left},
            device_id_type=MESH,
        )

    def ag_wait(way, s, u):
        chunk = (mz + nz - 1 - s) % nz if way == 0 else (mz + 1 + s) % nz
        ref = w_all.at[chunk, pl.ds(u * piece, piece), :]
        pltpu.make_async_copy(ref, ref, ag_rs.at[way, s, u]).wait()

    def pump(s):
        for u in range(SUB):
            for way, count in ((0, n_right), (1, n_left)):
                if 1 <= s <= count:
                    ag_wait(way, s - 1, u)
                if s < count:
                    ag_copy(way, s, u).start()

    last = n_right
    done = [0]

    def pump_to(s):
        while done[0] <= min(s, last):
            pump(done[0])
            done[0] += 1

    pump_to(0)

    def send_states(src, dst, which):
        def one(k, carry):
            to = shifted(k, 1)
            pltpu.make_async_remote_copy(
                src_ref=src.at[to],
                dst_ref=dst.at[ms],
                send_sem=p_sem.at[which, 0],
                recv_sem=p_sem.at[which, 1],
                device_id={"seq": to},
                device_id_type=MESH,
            ).start()
            return carry

        lax.fori_loop(1, ns, one, 0)

    def wait_bytes(ref, sem):
        pltpu.make_async_copy(ref, ref, sem).wait()

    send_states(st_send, st_recv, 0)
    st_recv[ms] = st_send[ms]

    causal = lax.broadcasted_iota(jnp.int32, (T, T), 0) >= lax.broadcasted_iota(
        jnp.int32, (T, T), 1
    )
    for h in range(H):
        sl = slice(h * HD, (h + 1) * HD)
        scores = dot(q_ref[0, :, sl], k_ref[0, :, sl], 1, 1)
        wq[h, :, 0:T] = jnp.where(causal, scores, 0.0).astype(BF16)

    eye = lax.broadcasted_iota(jnp.int32, (T, T), 0) == lax.broadcasted_iota(jnp.int32, (T, T), 1)
    ids = ids_ref[0].astype(F32)

    def as_col(row):
        return jnp.sum(jnp.where(eye, row, 0.0), axis=1, keepdims=True)

    id0, id1 = as_col(ids[0:1]).astype(jnp.int32), as_col(ids[1:2]).astype(jnp.int32)
    lane_e = lax.broadcasted_iota(jnp.int32, (T, n_exp), 1)
    hot0, hot1 = (lane_e == id0).astype(F32), (lane_e == id1).astype(F32)
    below = (
        lax.broadcasted_iota(jnp.int32, (T, T), 0) > lax.broadcasted_iota(jnp.int32, (T, T), 1)
    ).astype(F32)
    counts = dot(below.astype(BF16), (hot0 + hot1).astype(BF16))

    def as_row(col):
        return jnp.sum(jnp.where(eye, col, 0.0), axis=0, keepdims=True)

    def relative(ident):
        c, x, y = ident % nc, (ident // nc) % nx, ident // (nc * nx)
        return (((y - my + ny) % ny) * nx + (x - mx + nx) % nx) * nc + (c - mc + nc) % nc

    rank0 = jnp.sum(counts * hot0, axis=1, keepdims=True)
    rank1 = jnp.sum(counts * hot1, axis=1, keepdims=True)
    rel_e = relative(lax.broadcasted_iota(jnp.int32, (1, n_exp), 1)).astype(F32)
    rel0 = jnp.sum(rel_e * hot0, axis=1, keepdims=True)
    rel1 = jnp.sum(rel_e * hot1, axis=1, keepdims=True)
    code0, code1 = rel0 * RB + rank0, rel1 * RB + rank1
    row0, row1 = as_row(code0).astype(jnp.int32), as_row(code1).astype(jnp.int32)
    icode0, icode1 = code0.astype(jnp.int32), code1.astype(jnp.int32)

    for q in range(Q):
        nst[q * T : (q + 1) * T, :] = cot_ref[0, :, q * DQ : (q + 1) * DQ]
    r_iota = lax.broadcasted_iota(jnp.int32, (GB, T), 0)
    for g in range(groups):
        for q in range(Q):
            at = r_iota + (g * GB - q * slots)
            hit = (at == row0) | (at == row1)
            place[g, :, q * T : (q + 1) * T] = jnp.where(hit, 1.0, 0.0).astype(BF16)

    def fill(g, buf):
        got = dot(place[g], nst[...]).astype(BF16)
        buf[pl.ds(g * GR, GR)] = got.reshape(GR, RB, DQ)

    def send_slot(k, src, dst, ss, rs, sign):
        return pltpu.make_async_remote_copy(
            src_ref=src.at[k],
            dst_ref=dst.at[k],
            send_sem=ss,
            recv_sem=rs,
            device_id={"seq": shifted(k, sign)},
            device_id_type=MESH,
        )

    def send_group(g, src, dst, ss, rs, sign):
        for i in range(GR):
            if g * GR + i > 0:
                send_slot(g * GR + i, src, dst, ss, rs.at[g], sign).start()

    def group_ref(g, buf):
        first = 1 if g == 0 else 0
        return buf.at[pl.ds(g * GR + first, GR - first)]

    for g in range(groups):
        fill(g, c_send)

    pump_to(1)
    wait_bytes(st_recv.at[pl.ds(0, ns - 1)], p_sem.at[0, 1])
    acc = jnp.zeros((PR, HD), F32)
    for j in range(ns):
        pf_send[j] = acc.astype(BF16)
        acc = acc + st_recv[j].astype(F32)
    send_states(pf_send, pf_recv, 1)
    pf_recv[ms] = pf_send[ms]

    for g in range(groups):
        send_group(g, c_send, c_recv, c_ss, c_rs, 1)
    c_recv[0] = c_send[0]
    pump_to(2)

    wait_bytes(pf_recv.at[pl.ds(0, ns - 1)], p_sem.at[1, 1])
    squares = jnp.zeros((T, HD), F32)
    for h in range(H):
        sl = slice(h * HD, (h + 1) * HD)
        n = HD // PR
        prefix = pf_recv[h * n : (h + 1) * n].reshape(HD, HD)
        att = dot(wq[h], v_ref[0, :, sl]) + dot(q_ref[0, :, sl], prefix)
        att = att * lax.rsqrt(jnp.mean(att * att, axis=-1, keepdims=True) + EPS)
        one = res_ref[0, :, sl].astype(F32) + att * again_ref[:, sl]
        stream[:, sl] = one
        squares = squares + one * one
    scale = lax.rsqrt(jnp.sum(squares, axis=-1, keepdims=True) / D + EPS)
    pump_to(3)
    logits = jnp.zeros((T, n_exp), F32)
    for q in range(Q):
        cols = slice(q * DQ, (q + 1) * DQ)
        part = (stream[:, cols] * scale * mgain_ref[:, cols]).astype(BF16)
        nst[q * T : (q + 1) * T, :] = part
        logits = logits + dot(part, router_ref[:, cols], 1, 1)

    for g in range(groups):
        fill(g, x_send)
        send_group(g, x_send, x_recv, x_ss, x_rs, 1)
    x_recv[0] = x_send[0]

    sig0 = jax.nn.sigmoid(jnp.sum(hot0 * logits, axis=1, keepdims=True))
    sig1 = jax.nn.sigmoid(jnp.sum(hot1 * logits, axis=1, keepdims=True))
    gate0, gate1 = sig0 / (sig0 + sig1), sig1 / (sig0 + sig1)
    low = lax.broadcasted_iota(jnp.int32, (T, 128), 1) >= 64

    def two_parts(gate):
        high = gate.astype(BF16).astype(F32)
        return jnp.where(low, gate - high, high).astype(BF16)

    g_rows = lax.broadcasted_iota(jnp.int32, (ns * 16, T), 0)
    grow0 = as_row(rel0 * 16 + rank0).astype(jnp.int32)
    grow1 = as_row(rel1 * 16 + rank1).astype(jnp.int32)
    g_msg = dot(jnp.where(g_rows == grow0, 1.0, 0.0).astype(BF16), two_parts(gate0)) + dot(
        jnp.where(g_rows == grow1, 1.0, 0.0).astype(BF16), two_parts(gate1)
    )
    g_send[...] = g_msg.astype(BF16).reshape(ns, 16, 128)

    def send_gate(k, carry):
        send_slot(k, g_send, g_recv, g_sem.at[0], g_sem.at[1], 1).start()
        return carry

    lax.fori_loop(1, ns, send_gate, 0)
    g_recv[0] = g_send[0]
    pump_to(4)

    l_iota = lax.broadcasted_iota(jnp.int32, (T, GB), 1)
    for g in range(groups):
        for q in range(Q):
            at = l_iota + (g * GB - q * slots)
            val = jnp.where(at == icode0, gate0, 0.0) + jnp.where(at == icode1, gate1, 0.0)
            placeg[q * T : (q + 1) * T, g * GB : (g + 1) * GB] = val.astype(BF16)
    pump_to(5)

    o = lax.broadcasted_iota(jnp.int32, (GB, GB), 0)
    c = lax.broadcasted_iota(jnp.int32, (GB, GB), 1)
    want = ((o // slots) % GR) * RB + (o // GX) * slots + o % slots
    perm = (c == want).astype(F32).astype(BF16)

    def unpack(g, src, dst):
        got = dot(perm, src[pl.ds(g * GR, GR)].reshape(GB, DQ)).astype(BF16)
        for q in range(Q):
            dst[g * GX : (g + 1) * GX, q * DQ : (q + 1) * DQ] = got[q * GX : (q + 1) * GX, :]

    for g in range(groups):
        wait_bytes(group_ref(g, c_recv), c_rs.at[g])
        unpack(g, c_recv, cs)
    pump_to(6)
    for g in range(groups):
        wait_bytes(group_ref(g, x_recv), x_rs.at[g])
        unpack(g, x_recv, xs)
        if g == groups // 2:
            pump_to(7)
    wait_bytes(g_recv.at[pl.ds(1, ns - 1)], g_sem.at[1])
    o16 = lax.broadcasted_iota(jnp.int32, (GX, GR * 16), 0)
    c16 = lax.broadcasted_iota(jnp.int32, (GX, GR * 16), 1)
    pick = (c16 == (o16 // slots) * 16 + o16 % slots).astype(F32).astype(BF16)
    for g in range(groups):
        got = dot(pick, g_recv[pl.ds(g * GR, GR)].reshape(GR * 16, 128))
        gcol[g * GX : (g + 1) * GX, :] = got[:, 0:1] + got[:, 64:65]
    pump_to(last)

    KB = rows_z * 2

    def fwd(i, carry):
        cols = pl.ds(pl.multiple_of(i * KB, KB), KB)
        w = w_all[pl.ds(2 * i, 2)].reshape(KB, 3 * FF)
        pre[:, 0 : 2 * FF] += dot(xs[:, cols], w[:, 0 : 2 * FF])
        pre[:, 2 * FF : 3 * FF] += dot(cs[:, cols], w[:, 2 * FF : 3 * FF])
        return carry

    pre[...] = jnp.zeros_like(pre)
    lax.fori_loop(0, nz // 2, fwd, 0)
    pre_gate = pre[:, 0:FF]
    pre_up = pre[:, FF : 2 * FF]
    gates = gcol[...]
    d_hidden = pre[:, 2 * FF : 3 * FF] * gates
    sigma = jax.nn.sigmoid(pre_gate)
    act = pre_gate * sigma
    hidden = (act * pre_up).astype(BF16)
    hid[...] = hidden
    hidg[...] = (hidden.astype(F32) * gates).astype(BF16)
    dgu[:, 0:FF] = (d_hidden * pre_up * sigma * (1.0 + pre_gate * (1.0 - sigma))).astype(BF16)
    dgu[:, FF : 2 * FF] = (d_hidden * act).astype(BF16)

    half = rows_z // SUB

    def grad_of(chunk):
        cols = pl.ds(pl.multiple_of(chunk * rows_z, rows_z), rows_z)
        return dot(xs[:, cols], dgu[...], 0, 0), dot(cs[:, cols], hidg[...], 0, 0)

    def rs_copy(way, s, u):
        return pltpu.make_async_remote_copy(
            src_ref=rs_send.at[way, s, pl.ds(u * half, half)],
            dst_ref=rs_recv.at[way, s, pl.ds(u * half, half)],
            send_sem=rr_ss.at[way, s, u],
            recv_sem=rr_rs.at[way, s, u],
            device_id={"dp": right if way == 0 else left},
            device_id_type=MESH,
        )

    def rs_step(s):
        for way, count in ((0, n_right), (1, n_left)):
            if s >= count:
                continue
            chunk = (mz + n_right - s) % nz if way == 0 else (mz + nz - n_left + s) % nz
            a, b = grad_of(chunk)
            for u in range(SUB):
                rows = slice(u * half, (u + 1) * half)
                pa, pb = a[rows], b[rows]
                if s > 0:
                    rs_copy(way, s - 1, u).wait_recv()
                    pa = pa + rs_recv[way, s - 1, rows, 0 : 2 * FF].astype(F32)
                    pb = pb + rs_recv[way, s - 1, rows, 2 * FF : 3 * FF].astype(F32)
                rs_send[way, s, rows, 0 : 2 * FF] = pa.astype(BF16)
                rs_send[way, s, rows, 2 * FF : 3 * FF] = pb.astype(BF16)
                rs_copy(way, s, u).start()

    rs_step(0)

    for g in range(groups):
        h_g = hid[g * GX : (g + 1) * GX, :]
        parts = []
        for q in range(Q):
            n = nz // Q
            w_q = w_all[q * n : (q + 1) * n, :, 2 * FF : 3 * FF].reshape(DQ, FF)
            parts.append(dot(h_g, w_q, 1, 1).astype(BF16))
        stacked = jnp.concatenate(parts, axis=0)
        r_send[pl.ds(g * GR, GR)] = dot(perm, stacked, 0, 0).astype(BF16).reshape(GR, RB, DQ)
        send_group(g, r_send, r_recv, r_ss, r_rs, -1)
    r_recv[0] = r_send[0]

    for s in range(1, n_right):
        rs_step(s)
        if s == n_right // 2 + 1 or n_right < 4:
            if s == n_right // 2 + 1 or s == n_right - 1:
                for g in range(groups):
                    wait_bytes(group_ref(g, r_recv), r_rs.at[g])
                back = r_recv[...].reshape(ns * RB, DQ)
                for q in range(Q):
                    cols = slice(q * DQ, (q + 1) * DQ)
                    got = dot(placeg[q * T : (q + 1) * T, :], back)
                    mixed_ref[0, :, cols] = (stream[:, cols] + got).astype(BF16)

    a, b = grad_of(mz)
    flag = (train_ref[0] > 0).astype(F32)
    for u in range(SUB):
        rows = slice(u * half, (u + 1) * half)
        pa, pb = a[rows], b[rows]
        for way, count in ((1, n_left), (0, n_right)):
            rs_copy(way, count - 1, u).wait_recv()
            pa = pa + rs_recv[way, count - 1, rows, 0 : 2 * FF].astype(F32)
            pb = pb + rs_recv[way, count - 1, rows, 2 * FF : 3 * FF].astype(F32)
        gg_ref[0, rows, :] = pa[:, 0:FF] * flag
        gu_ref[0, rows, :] = pa[:, FF : 2 * FF] * flag
        gd_ref[0, rows, :] = pb * flag

    for way, count in ((0, n_right), (1, n_left)):
        for s in range(count):
            for u in range(SUB):
                ag_copy(way, s, u).wait_send()
                rs_copy(way, s, u).wait_send()
    for which in range(2):
        wait_bytes(st_send.at[pl.ds(0, ns - 1)], p_sem.at[which, 0])
    wait_bytes(c_send.at[pl.ds(1, ns - 1)], c_ss)
    wait_bytes(x_send.at[pl.ds(1, ns - 1)], x_ss)
    wait_bytes(g_send.at[pl.ds(1, ns - 1)], g_sem.at[0])
    wait_bytes(r_send.at[pl.ds(1, ns - 1)], r_ss)


def body(
    grid3,
    nz,
    queries,
    keys,
    values,
    residual_in,
    cotangent,
    expert_ids,
    router,
    attn_gain,
    moe_gain,
    w_gate,
    w_up,
    w_down,
    trainable,
):
    ns = grid3[0] * grid3[1] * grid3[2]
    T, D = queries.shape[1:]
    H = D // HD
    FF = w_gate.shape[2]
    slots = max(2, 3 * T // ns)
    rows_z = w_gate.shape[1]
    RB, DQ, R = Q * slots, D // Q, ns * slots
    PR = H * HD // ns
    groups = ns // GR
    n_right = nz // 2
    vm = pltpu.VMEM
    dma = pltpu.SemaphoreType.DMA
    scratch = [
        vm((nz, rows_z, 3 * FF), BF16),
        vm((ns, PR, HD), BF16),
        vm((ns, PR, HD), BF16),
        vm((ns, PR, HD), BF16),
        vm((ns, PR, HD), BF16),
        vm((H, T, T), BF16),
        vm((T, D), F32),
        vm((Q * T, DQ), BF16),
        vm((groups, GR * RB, Q * T), BF16),
        vm((Q * T, ns * RB), BF16),
        vm((ns, RB, DQ), BF16),
        vm((ns, RB, DQ), BF16),
        vm((ns, RB, DQ), BF16),
        vm((ns, RB, DQ), BF16),
        vm((ns, 16, 128), BF16),
        vm((ns, 16, 128), BF16),
        vm((R, D), BF16),
        vm((R, D), BF16),
        vm((R, 3 * FF), F32),
        vm((R, 1), F32),
        vm((R, 2 * FF), BF16),
        vm((R, FF), BF16),
        vm((R, FF), BF16),
        vm((ns, RB, DQ), BF16),
        vm((ns, RB, DQ), BF16),
        vm((2, n_right, rows_z, 3 * FF), BF16),
        vm((2, n_right, rows_z, 3 * FF), BF16),
        dma((2, n_right, SUB)),
        dma((2, n_right, SUB)),
        dma((2, 2)),
        dma(()),
        dma((groups,)),
        dma(()),
        dma((groups,)),
        dma((2,)),
        dma(()),
        dma((groups,)),
        dma((2, n_right, SUB)),
        dma((2, n_right, SUB)),
    ]
    in_vmem = pl.BlockSpec(memory_space=pltpu.VMEM)
    return pl.pallas_call(
        functools.partial(kernel, grid3, slots),
        out_shape=(
            jax.ShapeDtypeStruct((1, T, D), BF16),
            jax.ShapeDtypeStruct((1, rows_z, FF), F32),
            jax.ShapeDtypeStruct((1, rows_z, FF), F32),
            jax.ShapeDtypeStruct((1, rows_z, FF), F32),
        ),
        in_specs=[in_vmem] * 12 + [pl.BlockSpec(memory_space=pltpu.SMEM)],
        out_specs=(in_vmem,) * 4,
        scratch_shapes=scratch,
        compiler_params=pltpu.CompilerParams(
            collective_id=0, has_side_effects=True, vmem_limit_bytes=60 * 1024 * 1024
        ),
        name="layer",
    )(
        queries,
        keys,
        values,
        residual_in,
        cotangent,
        jnp.transpose(expert_ids, (0, 2, 1)),
        router.T,
        attn_gain.reshape(1, D),
        moe_gain.reshape(1, D),
        w_gate,
        w_up,
        w_down,
        trainable,
    )


def solution(mesh, grid3=(4, 4, 2)):
    blocks = P("dp", "seq", None)
    weights = P("seq", "dp", None)
    return jax.shard_map(
        functools.partial(body, grid3, mesh.shape["dp"]),
        mesh=mesh,
        in_specs=(blocks,) * 6 + (P(), P(), P()) + (weights,) * 3 + (P("seq"),),
        out_specs=(blocks, weights, weights, weights),
        check_vma=False,
    )
```

time: 291 us -> 131 us (0.45)
  the two profiles are of different devices: /device:TPU:4 before, /device:TPU:32 now
where the time goes in v1:
time: 131 us; the launch traced here: 130 us
  Pallas kernels  125 us (95%)
  local copies, waits for them, and re-layouts  4.48 us (3%)
    pallas_call x1, Pallas kernels, body(): pl.pallas_call(functools.partial(kernel, grid3, slots), out_shape=(jax.Sh...  125 us
    unnamed x10, local copies, waits for them, and re-layouts  4.48 us

profile of v1, /device:TPU:32, one launch (start us, length us, event | category | flops | bytes accessed | tf_op | source)
XLA Modules:
  0.0 130.4 jit_solution(4482951938522342082)
XLA Ops:
  1.3 124.6 %layer.1 = (bf16[1,128,2048]{2,1,0:T(8,128)(2,1)}, f32[1,128,256]{2,1,0:T(8,128)}, f32[1,128,256]{2,1,0:T(8,128)}, f32[1,128,256]{2,1,0:T(8,128)}) custom-call(bf16[1,128,2048]{2,1,0:T(8,128)(2,1)} %q_ref.1, bf16[1,128,2048]{2,1,0:T(8,128)(2,1)} %k_ref.1, bf16[1,128,2048]{2,1,0:T(8,128)(2,1)} %v_ref.1, bf16[1,128,2048]{2,1,0:T(8,128)(2,1)} %res_ref.1, ...), custom_call_target="tpu_custom_call" | custom-call | tf_op jit(solution)/shard_map/layer/pallas_call | solution.py:546
  125.9 0.0 copy-start.2
  125.9 1.9 %copy.22 = bf16[1,128,2048]{2,1,0:T(8,128)(2,1)} copy(bf16[1,128,2048]{2,1,0:T(8,128)(2,1)} %get-tuple-element.8) | data formatting | bytes 1048576
  127.8 0.0 copy-done.2
  127.8 0.0 copy-start.1
  127.8 0.7 copy.23
  128.5 0.3 copy-done.1
  128.8 0.0 copy-start
  128.8 0.7 copy.24
  129.4 0.3 copy-done
  129.7 0.7 copy.25
Async XLA Ops:
  125.9 1.9 %copy-start.2 = (f32[1,128,256]{2,1,0:T(8,128)S(1)}, f32[1,128,256]{2,1,0:T(8,128)}, u32[]{:S(2)}) copy-start(f32[1,128,256]{2,1,0:T(8,128)} %get-tuple-element.9) | copy-start | bytes 393220
  127.8 1.0 copy-start.1
  128.8 1.0 copy-start

commit v2 on v1

v2 whole, which is shorter than its diff:
```python
import functools

import jax
import jax.numpy as jnp
from jax import lax
from jax.experimental import pallas as pl
from jax.experimental.pallas import tpu as pltpu
from jax.sharding import PartitionSpec as P

HD = 128
EPS = 1e-06
MESH = pl.DeviceIdType.MESH
F32 = jnp.float32
BF16 = jnp.bfloat16
Q = 4
GR = 4
SUB = 2


def early(groups):
    return [[g for g in range(groups) if min(g * 8 // groups, 7) in at] for at in ((0,), (1, 2), (3, 4), (5, 6, 7))]


def dot(a, b, ca=1, cb=0):
    return lax.dot_general(a, b, (((ca,), (cb,)), ((), ())), preferred_element_type=F32)


def kernel(
    grid3,
    slots,
    q_in,
    k_in,
    v_in,
    res_in,
    cot_in,
    ids_ref,
    router_ref,
    again_ref,
    mgain_ref,
    wg_in,
    wu_in,
    wd_in,
    train_ref,
    mixed_ref,
    gg_ref,
    gu_ref,
    gd_ref,
    in_sem,
    q_ref,
    k_ref,
    v_ref,
    res_ref,
    cot_ref,
    w_all,
    st,
    sib,
    cs_send,
    cs_recv,
    pf_send,
    pf_recv,
    up_send,
    pfx,
    wq,
    stream,
    nst,
    place,
    placeg,
    c_send,
    c_recv,
    x_send,
    x_recv,
    g_send,
    g_recv,
    xs,
    cs,
    pre,
    gcol,
    dgu,
    hid,
    hidg,
    r_send,
    r_recv,
    gbuf,
    rs_send,
    rs_recv,
    ag_ss,
    ag_rs,
    p_sem,
    c_ss,
    c_rs,
    x_ss,
    x_rs,
    g_sem,
    r_ss,
    r_rs,
    rr_ss,
    rr_rs,
):
    ny, nx, nc = grid3
    ns = ny * nx * nc
    T, D = q_ref.shape
    H = D // HD
    DQ = D // Q
    FF = wg_in.shape[2]
    nz = w_all.shape[0]
    rows_z = w_all.shape[1]
    chips, PR = st.shape[1], st.shape[2]
    RB = Q * slots
    groups = ns // GR
    GB = GR * RB
    GX = GR * slots
    n_exp = router_ref.shape[0]

    mz = lax.axis_index("dp")
    ms = lax.axis_index("seq")
    mc = ms % nc
    mx = (ms // nc) % nx
    my = ms // (nc * nx)
    right, left = (mz + 1) % nz, (mz + nz - 1) % nz

    mchip = my * nx + mx

    def hops(p):
        dx, dy = (p // nc) % nx, p // (nc * nx)
        return min(dx, nx - dx) + min(dy, ny - dy)

    slot_list = [0] + sorted(range(1, ns), key=lambda p: -hops(p))

    def moved(p, sign):
        dc, dx, dy = p % nc, (p // nc) % nx, p // (nc * nx)
        c = (mc + sign * dc + nc) % nc
        x = (mx + sign * dx + nx) % nx
        y = (my + sign * dy + ny) % ny
        return (y * nx + x) * nc + c

    def shifted(k, sign):
        return moved(slot_list[k], sign)

    loads = {}
    for n, (name, src, dst) in enumerate(
        (
            ("k", k_in.at[0], k_ref),
            ("v", v_in.at[0], v_ref),
            ("gate", wg_in.at[0], w_all.at[mz, :, pl.ds(0, FF)]),
            ("up", wu_in.at[0], w_all.at[mz, :, pl.ds(FF, FF)]),
            ("down", wd_in.at[0], w_all.at[mz, :, pl.ds(2 * FF, FF)]),
            ("cot", cot_in.at[0], cot_ref),
            ("q", q_in.at[0], q_ref),
            ("res", res_in.at[0], res_ref),
        )
    ):
        loads[name] = pltpu.make_async_copy(src, dst, in_sem.at[n])
        loads[name].start()

    barrier = pltpu.get_barrier_semaphore()

    def greet(k, carry):
        pl.semaphore_signal(barrier, inc=1, device_id={"seq": moved(k, 1)}, device_id_type=MESH)
        return carry

    lax.fori_loop(1, ns, greet, 0)
    for z in (left, right):
        pl.semaphore_signal(barrier, inc=1, device_id={"dp": z}, device_id_type=MESH)

    for name in ("gate", "up", "down"):
        loads[name].wait()

    steps = nz // 2
    piece = rows_z // SUB
    near = (right, left)

    def order(way):
        return range(SUB) if way == 0 else range(SUB - 1, -1, -1)

    def far_half(way, u):
        return (u < SUB // 2) == (way == 0)

    def ag_copy(way, s, u):
        chunk = (mz + nz - s) % nz if way == 0 else (mz + s) % nz
        ref = w_all.at[chunk, pl.ds(u * piece, piece), :]
        return pltpu.make_async_remote_copy(
            src_ref=ref,
            dst_ref=ref,
            send_sem=ag_ss.at[way, s, u],
            recv_sem=ag_rs.at[way, s, u],
            device_id={"dp": near[way]},
            device_id_type=MESH,
        )

    def ag_wait(way, s, u):
        chunk = (mz + nz - 1 - s) % nz if way == 0 else (mz + 1 + s) % nz
        ref = w_all.at[chunk, pl.ds(u * piece, piece), :]
        pltpu.make_async_copy(ref, ref, ag_rs.at[way, s, u]).wait()

    def ag_used(way, s, u):
        return 0 <= s < steps and (s < steps - 1 or far_half(way, u))

    def pump(s, i):
        for way in (0, 1):
            u = order(way)[i]
            if ag_used(way, s - 1, u):
                ag_wait(way, s - 1, u)
            if ag_used(way, s, u):
                ag_copy(way, s, u).start()

    items = [(s, i) for s in range(steps + 1) for i in range(SUB)]

    def pump_to(s, i=SUB - 1):
        while items and items[0] <= (s, i):
            pump(*items.pop(0))

    loads["k"].wait()
    loads["v"].wait()
    n_piece = HD // PR
    for h in range(H):
        sl = slice(h * HD, (h + 1) * HD)
        state = dot(k_ref[:, sl], v_ref[:, sl], 0, 0).astype(BF16)
        for i in range(n_piece):
            p = h * n_piece + i
            st[p % nc, p // nc] = state[i * PR : (i + 1) * PR, :]

    pl.semaphore_wait(barrier, ns - 1 + 2)
    pump_to(0)

    sibling = mchip * nc + (1 - mc)
    pair_a = pltpu.make_async_remote_copy(
        src_ref=st.at[1 - mc],
        dst_ref=sib,
        send_sem=p_sem.at[0, 0],
        recv_sem=p_sem.at[0, 1],
        device_id={"seq": sibling},
        device_id_type=MESH,
    )
    pair_a.start()

    def wait_bytes(ref, sem):
        pltpu.make_async_copy(ref, ref, sem).wait()

    def send_pieces(src, dst, which):
        for p in sorted(range(1, chips), key=lambda p: -hops(p * nc)):
            to = moved(p * nc, 1)
            pltpu.make_async_remote_copy(
                src_ref=src.at[to // nc],
                dst_ref=dst.at[mchip],
                send_sem=p_sem.at[which, 0],
                recv_sem=p_sem.at[which, 1],
                device_id={"seq": to},
                device_id_type=MESH,
            ).start()

    eye = lax.broadcasted_iota(jnp.int32, (T, T), 0) == lax.broadcasted_iota(jnp.int32, (T, T), 1)
    ids = ids_ref[0].astype(F32)

    def as_col(row):
        return jnp.sum(jnp.where(eye, row, 0.0), axis=1, keepdims=True)

    id0, id1 = as_col(ids[0:1]).astype(jnp.int32), as_col(ids[1:2]).astype(jnp.int32)
    lane_e = lax.broadcasted_iota(jnp.int32, (T, n_exp), 1)
    hot0, hot1 = (lane_e == id0).astype(F32), (lane_e == id1).astype(F32)
    below = (
        lax.broadcasted_iota(jnp.int32, (T, T), 0) > lax.broadcasted_iota(jnp.int32, (T, T), 1)
    ).astype(F32)
    counts = dot(below.astype(BF16), (hot0 + hot1).astype(BF16))

    def as_row(col):
        return jnp.sum(jnp.where(eye, col, 0.0), axis=0, keepdims=True)

    def relative(ident):
        c, x, y = ident % nc, (ident // nc) % nx, ident // (nc * nx)
        return (((y - my + ny) % ny) * nx + (x - mx + nx) % nx) * nc + (c - mc + nc) % nc

    rank0 = jnp.sum(counts * hot0, axis=1, keepdims=True)
    rank1 = jnp.sum(counts * hot1, axis=1, keepdims=True)
    rel_n = relative(lax.broadcasted_iota(jnp.int32, (1, n_exp), 1))
    rel_e = jnp.zeros((1, n_exp), F32)
    for k in range(1, ns):
        rel_e = rel_e + jnp.where(rel_n == slot_list[k], float(k), 0.0)
    rel0 = jnp.sum(rel_e * hot0, axis=1, keepdims=True)
    rel1 = jnp.sum(rel_e * hot1, axis=1, keepdims=True)
    code0, code1 = rel0 * RB + rank0, rel1 * RB + rank1
    row0, row1 = as_row(code0).astype(jnp.int32), as_row(code1).astype(jnp.int32)
    icode0, icode1 = code0.astype(jnp.int32), code1.astype(jnp.int32)

    loads["cot"].wait()
    for q in range(Q):
        nst[q * T : (q + 1) * T, :] = cot_ref[:, q * DQ : (q + 1) * DQ]
    r_iota = lax.broadcasted_iota(jnp.int32, (GB, T), 0)
    for g in range(groups):
        for q in range(Q):
            at = r_iota + (g * GB - q * slots)
            hit = (at == row0) | (at == row1)
            place[g, :, q * T : (q + 1) * T] = jnp.where(hit, 1.0, 0.0).astype(BF16)

    pair_a.wait_recv()
    cs_send[...] = (st[mc].astype(F32) + sib[...].astype(F32)).astype(BF16)

    send_pieces(cs_send, cs_recv, 1)
    cs_recv[mchip] = cs_send[mchip]
    def fill(g, buf):
        got = dot(place[g], nst[...]).astype(BF16)
        buf[pl.ds(g * GR, GR)] = got.reshape(GR, RB, DQ)

    def send_slot(k, src, dst, ss, rs, sign):
        return pltpu.make_async_remote_copy(
            src_ref=src.at[k],
            dst_ref=dst.at[k],
            send_sem=ss,
            recv_sem=rs,
            device_id={"seq": shifted(k, sign)},
            device_id_type=MESH,
        )

    def send_group(g, src, dst, ss, rs, sign):
        for i in range(GR):
            if g * GR + i > 0:
                send_slot(g * GR + i, src, dst, ss, rs.at[g], sign).start()

    def group_ref(g, buf):
        first = 1 if g == 0 else 0
        return buf.at[pl.ds(g * GR + first, GR - first)]

    for g in range(groups):
        fill(g, c_send)
        if g in early(groups)[0]:
            send_group(g, c_send, c_recv, c_ss, c_rs, 1)
    pump_to(1, 0)
    for g in early(groups)[1]:
        send_group(g, c_send, c_recv, c_ss, c_rs, 1)

    loads["q"].wait()
    loads["res"].wait()
    causal = lax.broadcasted_iota(jnp.int32, (T, T), 0) >= lax.broadcasted_iota(
        jnp.int32, (T, T), 1
    )
    for h in range(H):
        sl = slice(h * HD, (h + 1) * HD)
        scores = dot(q_ref[:, sl], k_ref[:, sl], 1, 1)
        wq[h, :, 0:T] = jnp.where(causal, scores, 0.0).astype(BF16)

    pump_to(1)
    wait_bytes(cs_recv.at[pl.ds(0, chips - 1)], p_sem.at[1, 1])
    acc = jnp.zeros((PR, HD), F32)
    for j in range(chips):
        pf_send[j] = acc.astype(BF16)
        acc = acc + cs_recv[j].astype(F32)
    send_pieces(pf_send, pf_recv, 2)
    pf_recv[mchip] = pf_send[mchip]
    pump_to(2, 0)
    for g in early(groups)[2]:
        send_group(g, c_send, c_recv, c_ss, c_rs, 1)
    pump_to(2)

    second = mc.astype(F32)
    wait_bytes(pf_recv.at[pl.ds(0, chips - 1)], p_sem.at[2, 1])
    got = pf_recv[...].astype(F32)
    up_send[...] = (got + (1.0 - second) * st[mc].astype(F32)).astype(BF16)
    pair_b = pltpu.make_async_remote_copy(
        src_ref=up_send,
        dst_ref=pfx.at[mc],
        send_sem=p_sem.at[3, 0],
        recv_sem=p_sem.at[3, 1],
        device_id={"seq": sibling},
        device_id_type=MESH,
    )
    pair_b.start()
    pfx[mc] = (got + second * sib[...].astype(F32)).astype(BF16)
    for g in early(groups)[3]:
        send_group(g, c_send, c_recv, c_ss, c_rs, 1)
    c_recv[0] = c_send[0]
    pump_to(3, 0)
    pair_b.wait_recv()

    squares = jnp.zeros((T, HD), F32)
    for h in range(H):
        sl = slice(h * HD, (h + 1) * HD)
        ps = range(h * n_piece, (h + 1) * n_piece)
        prefix = jnp.concatenate([pfx[p % nc, p // nc] for p in ps], axis=0)
        att = dot(wq[h], v_ref[:, sl]) + dot(q_ref[:, sl], prefix)
        att = att * lax.rsqrt(jnp.mean(att * att, axis=-1, keepdims=True) + EPS)
        one = res_ref[:, sl].astype(F32) + att * again_ref[:, sl]
        stream[:, sl] = one
        squares = squares + one * one
        if h == H // 2:
            pump_to(3)
    scale = lax.rsqrt(jnp.sum(squares, axis=-1, keepdims=True) / D + EPS)
    logits = jnp.zeros((T, n_exp), F32)
    for q in range(Q):
        cols = slice(q * DQ, (q + 1) * DQ)
        part = (stream[:, cols] * scale * mgain_ref[:, cols]).astype(BF16)
        nst[q * T : (q + 1) * T, :] = part
        logits = logits + dot(part, router_ref[:, cols], 1, 1)
    pump_to(4, 0)

    for g in range(groups):
        fill(g, x_send)
        send_group(g, x_send, x_recv, x_ss, x_rs, 1)
    pump_to(4)
    x_recv[0] = x_send[0]

    sig0 = jax.nn.sigmoid(jnp.sum(hot0 * logits, axis=1, keepdims=True))
    sig1 = jax.nn.sigmoid(jnp.sum(hot1 * logits, axis=1, keepdims=True))
    gate0, gate1 = sig0 / (sig0 + sig1), sig1 / (sig0 + sig1)
    low = lax.broadcasted_iota(jnp.int32, (T, 128), 1) >= 64

    def two_parts(gate):
        high = gate.astype(BF16).astype(F32)
        return jnp.where(low, gate - high, high).astype(BF16)

    g_rows = lax.broadcasted_iota(jnp.int32, (ns * 16, T), 0)
    grow0 = as_row(rel0 * 16 + rank0).astype(jnp.int32)
    grow1 = as_row(rel1 * 16 + rank1).astype(jnp.int32)
    g_msg = dot(jnp.where(g_rows == grow0, 1.0, 0.0).astype(BF16), two_parts(gate0)) + dot(
        jnp.where(g_rows == grow1, 1.0, 0.0).astype(BF16), two_parts(gate1)
    )
    g_send[...] = g_msg.astype(BF16).reshape(ns, 16, 128)

    for k in range(1, ns):
        send_slot(k, g_send, g_recv, g_sem.at[0], g_sem.at[1], 1).start()
    g_recv[0] = g_send[0]
    pump_to(5, 0)

    l_iota = lax.broadcasted_iota(jnp.int32, (T, GB), 1)
    for g in range(groups):
        for q in range(Q):
            at = l_iota + (g * GB - q * slots)
            val = jnp.where(at == icode0, gate0, 0.0) + jnp.where(at == icode1, gate1, 0.0)
            placeg[q * T : (q + 1) * T, g * GB : (g + 1) * GB] = val.astype(BF16)
    pump_to(5)

    o = lax.broadcasted_iota(jnp.int32, (GB, GB), 0)
    c = lax.broadcasted_iota(jnp.int32, (GB, GB), 1)
    want = ((o // slots) % GR) * RB + (o // GX) * slots + o % slots
    perm = (c == want).astype(F32).astype(BF16)

    def unpack(g, src, dst):
        got = dot(perm, src[pl.ds(g * GR, GR)].reshape(GB, DQ)).astype(BF16)
        for q in range(Q):
            dst[g * GX : (g + 1) * GX, q * DQ : (q + 1) * DQ] = got[q * GX : (q + 1) * GX, :]

    KB = rows_z * 2

    def matmul_rows(src, rows, c0, c1):
        def one(i, carry):
            cols = pl.ds(pl.multiple_of(i * KB, KB), KB)
            w = w_all[pl.ds(2 * i, 2), :, c0:c1].reshape(KB, c1 - c0)
            pre[rows, c0:c1] += dot(src[rows, cols], w)
            return carry

        lax.fori_loop(0, nz // 2, one, 0)

    pre[...] = jnp.zeros_like(pre)
    for g in range(groups):
        wait_bytes(group_ref(g, c_recv), c_rs.at[g])
        unpack(g, c_recv, cs)
        if g == groups // 2:
            pump_to(6, 0)
    pump_to(6)
    first_half = groups // 2
    for g in range(first_half):
        wait_bytes(group_ref(g, x_recv), x_rs.at[g])
        unpack(g, x_recv, xs)
        if g == 0:
            pump_to(7, 0)
        elif g == first_half // 2:
            pump_to(7)
    pump_to(steps)
    cut = first_half * GX
    R = ns * slots
    matmul_rows(cs, slice(0, R), 2 * FF, 3 * FF)
    if cut:
        matmul_rows(xs, slice(0, cut), 0, 2 * FF)
    for g in range(first_half, groups):
        wait_bytes(group_ref(g, x_recv), x_rs.at[g])
        unpack(g, x_recv, xs)
    matmul_rows(xs, slice(cut, R), 0, 2 * FF)
    wait_bytes(g_recv.at[pl.ds(1, ns - 1)], g_sem.at[1])
    o16 = lax.broadcasted_iota(jnp.int32, (GX, GR * 16), 0)
    c16 = lax.broadcasted_iota(jnp.int32, (GX, GR * 16), 1)
    pick = (c16 == (o16 // slots) * 16 + o16 % slots).astype(F32).astype(BF16)
    for g in range(groups):
        got = dot(pick, g_recv[pl.ds(g * GR, GR)].reshape(GR * 16, 128))
        gcol[g * GX : (g + 1) * GX, :] = got[:, 0:1] + got[:, 64:65]

    pre_gate = pre[:, 0:FF]
    pre_up = pre[:, FF : 2 * FF]
    gates = gcol[...]
    d_hidden = pre[:, 2 * FF : 3 * FF] * gates
    sigma = jax.nn.sigmoid(pre_gate)
    act = pre_gate * sigma
    hidden = (act * pre_up).astype(BF16)
    hid[...] = hidden
    hidg[...] = (hidden.astype(F32) * gates).astype(BF16)
    dgu[:, 0:FF] = (d_hidden * pre_up * sigma * (1.0 + pre_gate * (1.0 - sigma))).astype(BF16)
    dgu[:, FF : 2 * FF] = (d_hidden * act).astype(BF16)

    half = rows_z // SUB

    def grad_of(chunk):
        cols = pl.ds(pl.multiple_of(chunk * rows_z, rows_z), rows_z)
        return dot(xs[:, cols], dgu[...], 0, 0), dot(cs[:, cols], hidg[...], 0, 0)

    def rs_copy(way, s, u):
        return pltpu.make_async_remote_copy(
            src_ref=rs_send.at[way, s, pl.ds(u * half, half)],
            dst_ref=rs_recv.at[way, s, pl.ds(u * half, half)],
            send_sem=rr_ss.at[way, s, u],
            recv_sem=rr_rs.at[way, s, u],
            device_id={"dp": near[way]},
            device_id_type=MESH,
        )

    def rs_used(way, s, u):
        return 0 <= s < steps and (s > 0 or far_half(way, u))

    def rs_order(way):
        return range(SUB - 1, -1, -1) if way == 0 else range(SUB)

    def rs_grads(s):
        for way in (0, 1):
            if way == 1 and s == 0:
                continue
            chunk = (mz + steps - s) % nz if way == 0 else (mz + nz - steps + s) % nz
            a, b = grad_of(chunk)
            gbuf[way, :, 0 : 2 * FF] = a
            gbuf[way, :, 2 * FF : 3 * FF] = b

    def rs_piece(way, s, u):
        rows = slice(u * half, (u + 1) * half)
        val = gbuf[0 if s == 0 else way, rows, :]
        if rs_used(way, s - 1, u):
            rs_copy(way, s - 1, u).wait_recv()
            val = val + rs_recv[way, s - 1, rows, :].astype(F32)
        rs_send[way, s, rows, :] = val.astype(BF16)
        rs_copy(way, s, u).start()

    def rs_pieces(s, when):
        for i in range(SUB):
            for way in (0, 1):
                u = rs_order(way)[i]
                if rs_used(way, s, u) and when(rs_used(way, s - 1, u)):
                    rs_piece(way, s, u)

    def always(waits):
        return True

    rs_grads(0)
    rs_pieces(0, always)
    rs_grads(1)
    rs_pieces(1, lambda waits: not waits)

    for g in range(groups):
        h_g = hid[g * GX : (g + 1) * GX, :]
        parts = []
        for q in range(Q):
            n = nz // Q
            w_q = w_all[q * n : (q + 1) * n, :, 2 * FF : 3 * FF].reshape(DQ, FF)
            parts.append(dot(h_g, w_q, 1, 1).astype(BF16))
        stacked = jnp.concatenate(parts, axis=0)
        r_send[pl.ds(g * GR, GR)] = dot(perm, stacked, 0, 0).astype(BF16).reshape(GR, RB, DQ)
        send_group(g, r_send, r_recv, r_ss, r_rs, -1)
    r_recv[0] = r_send[0]

    rs_pieces(1, lambda waits: waits)

    for s in range(2, steps + 1):
        if s < steps:
            rs_grads(s)
            rs_pieces(s, always)
        if s == (5 if steps > 5 else steps):
            for g in range(groups):
                wait_bytes(group_ref(g, r_recv), r_rs.at[g])
            back = r_recv[...].reshape(ns * RB, DQ)
            for q in range(Q):
                cols = slice(q * DQ, (q + 1) * DQ)
                got = dot(placeg[q * T : (q + 1) * T, :], back)
                mixed_ref[0, :, cols] = (stream[:, cols] + got).astype(BF16)

    a, b = grad_of(mz)
    gbuf[0, :, 0 : 2 * FF] = a
    gbuf[0, :, 2 * FF : 3 * FF] = b
    flag = (train_ref[0] > 0).astype(F32)
    for way in (0, 1):
        for u in rs_order(way):
            rows = slice(u * half, (u + 1) * half)
            rs_copy(way, steps - 1, u).wait_recv()
            gbuf[0, rows, :] = gbuf[0, rows, :] + rs_recv[way, steps - 1, rows, :].astype(F32)
    gg_ref[0] = gbuf[0, :, 0:FF] * flag
    gu_ref[0] = gbuf[0, :, FF : 2 * FF] * flag
    gd_ref[0] = gbuf[0, :, 2 * FF : 3 * FF] * flag

    for way in (0, 1):
        for s in range(steps):
            for u in range(SUB):
                if ag_used(way, s, u):
                    ag_copy(way, s, u).wait_send()
                if rs_used(way, s, u):
                    rs_copy(way, s, u).wait_send()
    pair_a.wait_send()
    pair_b.wait_send()
    wait_bytes(cs_send.at[pl.ds(0, chips - 1)], p_sem.at[1, 0])
    wait_bytes(pf_send.at[pl.ds(0, chips - 1)], p_sem.at[2, 0])
    wait_bytes(c_send.at[pl.ds(1, ns - 1)], c_ss)
    wait_bytes(x_send.at[pl.ds(1, ns - 1)], x_ss)
    wait_bytes(g_send.at[pl.ds(1, ns - 1)], g_sem.at[0])
    wait_bytes(r_send.at[pl.ds(1, ns - 1)], r_ss)


def body(
    grid3,
    nz,
    queries,
    keys,
    values,
    residual_in,
    cotangent,
    expert_ids,
    router,
    attn_gain,
    moe_gain,
    w_gate,
    w_up,
    w_down,
    trainable,
):
    ns = grid3[0] * grid3[1] * grid3[2]
    T, D = queries.shape[1:]
    H = D // HD
    FF = w_gate.shape[2]
    slots = max(2, 3 * T // ns)
    rows_z = w_gate.shape[1]
    RB, DQ, R = Q * slots, D // Q, ns * slots
    PR = H * HD // ns
    groups = ns // GR
    steps = nz // 2
    nc = grid3[2]
    chips = ns // nc
    vm = pltpu.VMEM
    dma = pltpu.SemaphoreType.DMA
    scratch = [
        dma((8,)),
        vm((T, D), BF16),
        vm((T, D), BF16),
        vm((T, D), BF16),
        vm((T, D), BF16),
        vm((T, D), BF16),
        vm((nz, rows_z, 3 * FF), BF16),
        vm((nc, chips, PR, HD), BF16),
        vm((chips, PR, HD), BF16),
        vm((chips, PR, HD), BF16),
        vm((chips, PR, HD), BF16),
        vm((chips, PR, HD), BF16),
        vm((chips, PR, HD), BF16),
        vm((chips, PR, HD), BF16),
        vm((nc, chips, PR, HD), BF16),
        vm((H, T, T), BF16),
        vm((T, D), F32),
        vm((Q * T, DQ), BF16),
        vm((groups, GR * RB, Q * T), BF16),
        vm((Q * T, ns * RB), BF16),
        vm((ns, RB, DQ), BF16),
        vm((ns, RB, DQ), BF16),
        vm((ns, RB, DQ), BF16),
        vm((ns, RB, DQ), BF16),
        vm((ns, 16, 128), BF16),
        vm((ns, 16, 128), BF16),
        vm((R, D), BF16),
        vm((R, D), BF16),
        vm((R, 3 * FF), F32),
        vm((R, 1), F32),
        vm((R, 2 * FF), BF16),
        vm((R, FF), BF16),
        vm((R, FF), BF16),
        vm((ns, RB, DQ), BF16),
        vm((ns, RB, DQ), BF16),
        vm((2, rows_z, 3 * FF), F32),
        vm((2, steps, rows_z, 3 * FF), BF16),
        vm((2, steps, rows_z, 3 * FF), BF16),
        dma((2, steps, SUB)),
        dma((2, steps, SUB)),
        dma((4, 2)),
        dma(()),
        dma((groups,)),
        dma(()),
        dma((groups,)),
        dma((2,)),
        dma(()),
        dma((groups,)),
        dma((2, steps, SUB)),
        dma((2, steps, SUB)),
    ]
    anywhere = pl.BlockSpec(memory_space=pl.ANY)
    in_vmem = pl.BlockSpec(memory_space=pltpu.VMEM)
    return pl.pallas_call(
        functools.partial(kernel, grid3, slots),
        out_shape=(
            pltpu.VMEM((1, T, D), BF16),
            pltpu.VMEM((1, rows_z, FF), F32),
            pltpu.VMEM((1, rows_z, FF), F32),
            pltpu.VMEM((1, rows_z, FF), F32),
        ),
        in_specs=[anywhere] * 5
        + [in_vmem] * 4
        + [anywhere] * 3
        + [pl.BlockSpec(memory_space=pltpu.SMEM)],
        out_specs=(in_vmem,) * 4,
        scratch_shapes=scratch,
        compiler_params=pltpu.CompilerParams(
            collective_id=0, has_side_effects=True, vmem_limit_bytes=60 * 1024 * 1024
        ),
        name="layer",
    )(
        queries,
        keys,
        values,
        residual_in,
        cotangent,
        jnp.transpose(expert_ids, (0, 2, 1)),
        router.T,
        attn_gain.reshape(1, D),
        moe_gain.reshape(1, D),
        w_gate,
        w_up,
        w_down,
        trainable,
    )


def solution(mesh, grid3=(4, 4, 2)):
    blocks = P("dp", "seq", None)
    weights = P("seq", "dp", None)
    return jax.shard_map(
        functools.partial(body, grid3, mesh.shape["dp"]),
        mesh=mesh,
        in_specs=(blocks,) * 6 + (P(), P(), P()) + (weights,) * 3 + (P("seq"),),
        out_specs=(blocks, weights, weights, weights),
        check_vma=False,
    )
```

time: 131 us -> 113 us (0.86)
  the two profiles are of different devices: /device:TPU:32 before, /device:TPU:26 now
where the time goes in v2:
time: 113 us
  Pallas kernels  109 us (96%)
  local copies, waits for them, and re-layouts  2.76 us (2%)
  between operations  1.29 us (1%)
    pallas_call x1, Pallas kernels, body(): pl.pallas_call(functools.partial(kernel, grid3, slots), out_shape=(pltpu....  109 us
    unnamed x4, local copies, waits for them, and re-layouts  2.76 us

profile of v2, /device:TPU:26, one launch (start us, length us, event | category | flops | bytes accessed | tf_op | source)
XLA Modules:
  0.0 112.9 jit_solution(4377803523661688197)
XLA Ops:
  1.3 108.9 %layer.1 = (bf16[1,128,2048]{2,1,0:T(8,128)(2,1)S(1)}, f32[1,128,256]{2,1,0:T(8,128)S(1)}, f32[1,128,256]{2,1,0:T(8,128)S(1)}, f32[1,128,256]{2,1,0:T(8,128)S(1)}) custom-call(bf16[1,128,2048]{2,1,0:T(8,128)(2,1)} %q_in.1, bf16[1,128,2048]{2,1,0:T(8,128)(2,1)} %k_in.1, bf16[1,128,2048]{2,1,0:T(8,128)(2,1)} %v_in.1, bf16[1,128,2048]{2,1,0:T(8,128)(2,1)} %res_in.1, ...), custom_call_target="tpu_custom_call" | custom-call | tf_op jit(solution)/shard_map/layer/pallas_call | solution.py:693
  110.2 0.8 copy.21
  111.0 0.7 copy.22
  111.6 0.7 copy.23
  112.3 0.7 copy.24

commit v3 on v2

--- a/solution.py
+++ b/solution.py
@@ -17,8 +17,11 @@
 SUB = 2
 
 
+EARLY = ((), (), (), (0, 1, 2, 3, 4, 5, 6, 7))
+
+
 def early(groups):
-    return [[g for g in range(groups) if min(g * 8 // groups, 7) in at] for at in ((0,), (1, 2), (3, 4), (5, 6, 7))]
+    return [[g for g in range(groups) if g * 8 // groups in at] for at in EARLY]
 
 
 def dot(a, b, ca=1, cb=0):
@@ -60,7 +63,6 @@
     pf_recv,
     up_send,
     pfx,
-    wq,
     stream,
     nst,
     place,
@@ -80,6 +82,7 @@
     hidg,
     r_send,
     r_recv,
+    eo,
     gbuf,
     rs_send,
     rs_recv,
@@ -219,6 +222,101 @@
             p = h * n_piece + i
             st[p % nc, p // nc] = state[i * PR : (i + 1) * PR, :]
 
+    eye = lax.broadcasted_iota(jnp.int32, (T, T), 0) == lax.broadcasted_iota(jnp.int32, (T, T), 1)
+    ids = ids_ref[0].astype(F32)
+
+    def as_col(row):
+        return jnp.sum(jnp.where(eye, row, 0.0), axis=1, keepdims=True)
+
+    id0, id1 = as_col(ids[0:1]).astype(jnp.int32), as_col(ids[1:2]).astype(jnp.int32)
+    lane_e = lax.broadcasted_iota(jnp.int32, (T, n_exp), 1)
+    hot0, hot1 = (lane_e == id0).astype(F32), (lane_e == id1).astype(F32)
+    below = (
+        lax.broadcasted_iota(jnp.int32, (T, T), 0) > lax.broadcasted_iota(jnp.int32, (T, T), 1)
+    ).astype(F32)
+    counts = dot(below.astype(BF16), (hot0 + hot1).astype(BF16))
+
+    def as_row(col):
+        return jnp.sum(jnp.where(eye, col, 0.0), axis=0, keepdims=True)
+
+    def relative(ident):
+        c, x, y = ident % nc, (ident // nc) % nx, ident // (nc * nx)
+        return (((y - my + ny) % ny) * nx + (x - mx + nx) % nx) * nc + (c - mc + nc) % nc
+
+    rank0 = jnp.sum(counts * hot0, axis=1, keepdims=True)
+    rank1 = jnp.sum(counts * hot1, axis=1, keepdims=True)
+    rel_n = relative(lax.broadcasted_iota(jnp.int32, (1, n_exp), 1))
+    rel_e = jnp.zeros((1, n_exp), F32)
+    for k in range(1, ns):
+        rel_e = rel_e + jnp.where(rel_n == slot_list[k], float(k), 0.0)
+    rel0 = jnp.sum(rel_e * hot0, axis=1, keepdims=True)
+    rel1 = jnp.sum(rel_e * hot1, axis=1, keepdims=True)
+    code0, code1 = rel0 * RB + rank0, rel1 * RB + rank1
+    row0, row1 = as_row(code0).astype(jnp.int32), as_row(code1).astype(jnp.int32)
+    icode0, icode1 = code0.astype(jnp.int32), code1.astype(jnp.int32)
+
+    loads["cot"].wait()
+    for q in range(Q):
+        nst[q * T : (q + 1) * T, :] = cot_ref[:, q * DQ : (q + 1) * DQ]
+    r_iota = lax.broadcasted_iota(jnp.int32, (GB, T), 0)
+    for g in range(groups):
+        for q in range(Q):
+            at = r_iota + (g * GB - q * slots)
+            hit = (at == row0) | (at == row1)
+            place[g, :, q * T : (q + 1) * T] = jnp.where(hit, 1.0, 0.0).astype(BF16)
+
+    half_g = max(1, groups // 2)
+
+    def fill(part, buf):
+        rows = place[pl.ds(part * half_g, half_g)].reshape(half_g * GB, Q * T)
+        got = dot(rows, nst[...]).astype(BF16)
+        buf[pl.ds(part * half_g * GR, half_g * GR)] = got.reshape(half_g * GR, RB, DQ)
+
+    def send_slot(k, src, dst, ss, rs, sign):
+        return pltpu.make_async_remote_copy(
+            src_ref=src.at[k],
+            dst_ref=dst.at[k],
+            send_sem=ss,
+            recv_sem=rs,
+            device_id={"seq": shifted(k, sign)},
+            device_id_type=MESH,
+        )
+
+    def send_group(g, src, dst, ss, rs, sign):
+        for i in range(GR):
+            if g * GR + i > 0:
+                send_slot(g * GR + i, src, dst, ss, rs.at[g], sign).start()
+
+    def group_ref(g, buf):
+        first = 1 if g == 0 else 0
+        return buf.at[pl.ds(g * GR + first, GR - first)]
+
+    for part in range(groups // half_g):
+        fill(part, c_send)
+
+    g_rows = lax.broadcasted_iota(jnp.int32, (ns * 16, T), 0)
+    grow0 = as_row(rel0 * 16 + rank0).astype(jnp.int32)
+    grow1 = as_row(rel1 * 16 + rank1).astype(jnp.int32)
+
+    def wide(col):
+        return jnp.broadcast_to(col.astype(F32), (T, 128)).astype(BF16)
+
+    g_msg = dot(jnp.where(g_rows == grow0, 1.0, 0.0).astype(BF16), wide(id1)) + dot(
+        jnp.where(g_rows == grow1, 1.0, 0.0).astype(BF16), wide(id0)
+    )
+    g_send[...] = g_msg.astype(BF16).reshape(ns, 16, 128)
+
+    loads["q"].wait()
+    causal = lax.broadcasted_iota(jnp.int32, (T, T), 0) >= lax.broadcasted_iota(
+        jnp.int32, (T, T), 1
+    )
+    for h in range(H):
+        sl = slice(h * HD, (h + 1) * HD)
+        scores = dot(q_ref[:, sl], k_ref[:, sl], 1, 1)
+        weights = jnp.where(causal, scores, 0.0).astype(BF16)
+        stream[:, sl] = dot(weights, v_ref[:, sl])
+    loads["res"].wait()
+
     pl.semaphore_wait(barrier, ns - 1 + 2)
     pump_to(0)
 
@@ -232,6 +330,11 @@
         device_id_type=MESH,
     )
     pair_a.start()
+    for g in early(groups)[0]:
+        send_group(g, c_send, c_recv, c_ss, c_rs, 1)
+    for k in range(1, ns):
+        send_slot(k, g_send, g_recv, g_sem.at[0], g_sem.at[1], 1).start()
+    g_recv[0] = g_send[0]
 
     def wait_bytes(ref, sem):
         pltpu.make_async_copy(ref, ref, sem).wait()
@@ -248,94 +351,14 @@
                 device_id_type=MESH,
             ).start()
 
-    eye = lax.broadcasted_iota(jnp.int32, (T, T), 0) == lax.broadcasted_iota(jnp.int32, (T, T), 1)
-    ids = ids_ref[0].astype(F32)
-
-    def as_col(row):
-        return jnp.sum(jnp.where(eye, row, 0.0), axis=1, keepdims=True)
-
-    id0, id1 = as_col(ids[0:1]).astype(jnp.int32), as_col(ids[1:2]).astype(jnp.int32)
-    lane_e = lax.broadcasted_iota(jnp.int32, (T, n_exp), 1)
-    hot0, hot1 = (lane_e == id0).astype(F32), (lane_e == id1).astype(F32)
-    below = (
-        lax.broadcasted_iota(jnp.int32, (T, T), 0) > lax.broadcasted_iota(jnp.int32, (T, T), 1)
-    ).astype(F32)
-    counts = dot(below.astype(BF16), (hot0 + hot1).astype(BF16))
-
-    def as_row(col):
-        return jnp.sum(jnp.where(eye, col, 0.0), axis=0, keepdims=True)
-
-    def relative(ident):
-        c, x, y = ident % nc, (ident // nc) % nx, ident // (nc * nx)
-        return (((y - my + ny) % ny) * nx + (x - mx + nx) % nx) * nc + (c - mc + nc) % nc
-
-    rank0 = jnp.sum(counts * hot0, axis=1, keepdims=True)
-    rank1 = jnp.sum(counts * hot1, axis=1, keepdims=True)
-    rel_n = relative(lax.broadcasted_iota(jnp.int32, (1, n_exp), 1))
-    rel_e = jnp.zeros((1, n_exp), F32)
-    for k in range(1, ns):
-        rel_e = rel_e + jnp.where(rel_n == slot_list[k], float(k), 0.0)
-    rel0 = jnp.sum(rel_e * hot0, axis=1, keepdims=True)
-    rel1 = jnp.sum(rel_e * hot1, axis=1, keepdims=True)
-    code0, code1 = rel0 * RB + rank0, rel1 * RB + rank1
-    row0, row1 = as_row(code0).astype(jnp.int32), as_row(code1).astype(jnp.int32)
-    icode0, icode1 = code0.astype(jnp.int32), code1.astype(jnp.int32)
-
-    loads["cot"].wait()
-    for q in range(Q):
-        nst[q * T : (q + 1) * T, :] = cot_ref[:, q * DQ : (q + 1) * DQ]
-    r_iota = lax.broadcasted_iota(jnp.int32, (GB, T), 0)
-    for g in range(groups):
-        for q in range(Q):
-            at = r_iota + (g * GB - q * slots)
-            hit = (at == row0) | (at == row1)
-            place[g, :, q * T : (q + 1) * T] = jnp.where(hit, 1.0, 0.0).astype(BF16)
-
     pair_a.wait_recv()
     cs_send[...] = (st[mc].astype(F32) + sib[...].astype(F32)).astype(BF16)
 
     send_pieces(cs_send, cs_recv, 1)
     cs_recv[mchip] = cs_send[mchip]
-    def fill(g, buf):
-        got = dot(place[g], nst[...]).astype(BF16)
-        buf[pl.ds(g * GR, GR)] = got.reshape(GR, RB, DQ)
-
-    def send_slot(k, src, dst, ss, rs, sign):
-        return pltpu.make_async_remote_copy(
-            src_ref=src.at[k],
-            dst_ref=dst.at[k],
-            send_sem=ss,
-            recv_sem=rs,
-            device_id={"seq": shifted(k, sign)},
-            device_id_type=MESH,
-        )
-
-    def send_group(g, src, dst, ss, rs, sign):
-        for i in range(GR):
-            if g * GR + i > 0:
-                send_slot(g * GR + i, src, dst, ss, rs.at[g], sign).start()
-
-    def group_ref(g, buf):
-        first = 1 if g == 0 else 0
-        return buf.at[pl.ds(g * GR + first, GR - first)]
-
-    for g in range(groups):
-        fill(g, c_send)
-        if g in early(groups)[0]:
-            send_group(g, c_send, c_recv, c_ss, c_rs, 1)
     pump_to(1, 0)
     for g in early(groups)[1]:
         send_group(g, c_send, c_recv, c_ss, c_rs, 1)
-
-    loads["q"].wait()
-    loads["res"].wait()
-    causal = lax.broadcasted_iota(jnp.int32, (T, T), 0) >= lax.broadcasted_iota(
-        jnp.int32, (T, T), 1
-    )
-    for h in range(H):
-        sl = slice(h * HD, (h + 1) * HD)
-        scores = dot(q_ref[:, sl], k_ref[:, sl], 1, 1)
-        wq[h, :, 0:T] = jnp.where(causal, scores, 0.0).astype(BF16)
 
     pump_to(1)
     wait_bytes(cs_recv.at[pl.ds(0, chips - 1)], p_sem.at[1, 1])
@@ -375,7 +398,7 @@
         sl = slice(h * HD, (h + 1) * HD)
         ps = range(h * n_piece, (h + 1) * n_piece)
         prefix = jnp.concatenate([pfx[p % nc, p // nc] for p in ps], axis=0)
-        att = dot(wq[h], v_ref[:, sl]) + dot(q_ref[:, sl], prefix)
+        att = stream[:, sl] + dot(q_ref[:, sl], prefix)
         att = att * lax.rsqrt(jnp.mean(att * att, axis=-1, keepdims=True) + EPS)
         one = res_ref[:, sl].astype(F32) + att * again_ref[:, sl]
         stream[:, sl] = one
@@ -391,32 +414,16 @@
         logits = logits + dot(part, router_ref[:, cols], 1, 1)
     pump_to(4, 0)
 
-    for g in range(groups):
-        fill(g, x_send)
-        send_group(g, x_send, x_recv, x_ss, x_rs, 1)
+    for part in range(groups // half_g):
+        fill(part, x_send)
+        for g in range(part * half_g, (part + 1) * half_g):
+            send_group(g, x_send, x_recv, x_ss, x_rs, 1)
     pump_to(4)
     x_recv[0] = x_send[0]
 
     sig0 = jax.nn.sigmoid(jnp.sum(hot0 * logits, axis=1, keepdims=True))
     sig1 = jax.nn.sigmoid(jnp.sum(hot1 * logits, axis=1, keepdims=True))
     gate0, gate1 = sig0 / (sig0 + sig1), sig1 / (sig0 + sig1)
-    low = lax.broadcasted_iota(jnp.int32, (T, 128), 1) >= 64
-
-    def two_parts(gate):
-        high = gate.astype(BF16).astype(F32)
-        return jnp.where(low, gate - high, high).astype(BF16)
-
-    g_rows = lax.broadcasted_iota(jnp.int32, (ns * 16, T), 0)
-    grow0 = as_row(rel0 * 16 + rank0).astype(jnp.int32)
-    grow1 = as_row(rel1 * 16 + rank1).astype(jnp.int32)
-    g_msg = dot(jnp.where(g_rows == grow0, 1.0, 0.0).astype(BF16), two_parts(gate0)) + dot(
-        jnp.where(g_rows == grow1, 1.0, 0.0).astype(BF16), two_parts(gate1)
-    )
-    g_send[...] = g_msg.astype(BF16).reshape(ns, 16, 128)
-
-    for k in range(1, ns):
-        send_slot(k, g_send, g_recv, g_sem.at[0], g_sem.at[1], 1).start()
-    g_recv[0] = g_send[0]
     pump_to(5, 0)
 
     l_iota = lax.broadcasted_iota(jnp.int32, (T, GB), 1)
@@ -448,42 +455,46 @@
 
         lax.fori_loop(0, nz // 2, one, 0)
 
+    pump_to(steps)
     pre[...] = jnp.zeros_like(pre)
-    for g in range(groups):
-        wait_bytes(group_ref(g, c_recv), c_rs.at[g])
-        unpack(g, c_recv, cs)
-        if g == groups // 2:
-            pump_to(6, 0)
-    pump_to(6)
-    first_half = groups // 2
-    for g in range(first_half):
-        wait_bytes(group_ref(g, x_recv), x_rs.at[g])
-        unpack(g, x_recv, xs)
-        if g == 0:
-            pump_to(7, 0)
-        elif g == first_half // 2:
-            pump_to(7)
-    pump_to(steps)
-    cut = first_half * GX
-    R = ns * slots
-    matmul_rows(cs, slice(0, R), 2 * FF, 3 * FF)
-    if cut:
-        matmul_rows(xs, slice(0, cut), 0, 2 * FF)
-    for g in range(first_half, groups):
-        wait_bytes(group_ref(g, x_recv), x_rs.at[g])
-        unpack(g, x_recv, xs)
-    matmul_rows(xs, slice(cut, R), 0, 2 * FF)
     wait_bytes(g_recv.at[pl.ds(1, ns - 1)], g_sem.at[1])
     o16 = lax.broadcasted_iota(jnp.int32, (GX, GR * 16), 0)
     c16 = lax.broadcasted_iota(jnp.int32, (GX, GR * 16), 1)
     pick = (c16 == (o16 // slots) * 16 + o16 % slots).astype(F32).astype(BF16)
     for g in range(groups):
         got = dot(pick, g_recv[pl.ds(g * GR, GR)].reshape(GR * 16, 128))
-        gcol[g * GX : (g + 1) * GX, :] = got[:, 0:1] + got[:, 64:65]
-
+        gcol[g * GX : (g + 1) * GX, :] = got[:, 0:1]
+    for g in range(groups):
+        wait_bytes(group_ref(g, c_recv), c_rs.at[g])
+        unpack(g, c_recv, cs)
+    R = ns * slots
+    matmul_rows(cs, slice(0, R), 2 * FF, 3 * FF)
+    first_half = groups // 2
+    for g in range(first_half):
+        wait_bytes(group_ref(g, x_recv), x_rs.at[g])
+        unpack(g, x_recv, xs)
+    cut = first_half * GX
+
+    def row_gates(a, b):
+        lane_r = lax.broadcasted_iota(jnp.int32, (b - a, n_exp), 1)
+        row_logits = dot(xs[a:b, :], router_ref[...], 1, 1)
+        own = jnp.sum(jnp.where(lane_r == ms, row_logits, 0.0), axis=1, keepdims=True)
+        hit = lane_r.astype(F32) == gcol[a:b, :]
+        other = jnp.sum(jnp.where(hit, row_logits, 0.0), axis=1, keepdims=True)
+        own, other = jax.nn.sigmoid(own), jax.nn.sigmoid(other)
+        gcol[a:b, :] = own / (own + other)
+
+    if cut:
+        matmul_rows(xs, slice(0, cut), 0, 2 * FF)
+        row_gates(0, cut)
+    for g in range(first_half, groups):
+        wait_bytes(group_ref(g, x_recv), x_rs.at[g])
+        unpack(g, x_recv, xs)
+    matmul_rows(xs, slice(cut, R), 0, 2 * FF)
+    row_gates(cut, R)
+    gates = gcol[...]
     pre_gate = pre[:, 0:FF]
     pre_up = pre[:, FF : 2 * FF]
-    gates = gcol[...]
     d_hidden = pre[:, 2 * FF : 3 * FF] * gates
     sigma = jax.nn.sigmoid(pre_gate)
     act = pre_gate * sigma
@@ -516,13 +527,17 @@
         return range(SUB - 1, -1, -1) if way == 0 else range(SUB)
 
     def rs_grads(s):
-        for way in (0, 1):
-            if way == 1 and s == 0:
-                continue
-            chunk = (mz + steps - s) % nz if way == 0 else (mz + nz - steps + s) % nz
-            a, b = grad_of(chunk)
-            gbuf[way, :, 0 : 2 * FF] = a
-            gbuf[way, :, 2 * FF : 3 * FF] = b
+        at = [
+            pl.ds(pl.multiple_of(chunk * rows_z, rows_z), rows_z)
+            for chunk in ((mz + steps - s) % nz, (mz + nz - steps + s) % nz)
+        ]
+        if s == 0:
+            at = at[:1]
+        a = dot(jnp.concatenate([xs[:, c] for c in at], axis=1), dgu[...], 0, 0)
+        b = dot(jnp.concatenate([cs[:, c] for c in at], axis=1), hidg[...], 0, 0)
+        for way in range(len(at)):
+            gbuf[way, :, 0 : 2 * FF] = a[way * rows_z : (way + 1) * rows_z]
+            gbuf[way, :, 2 * FF : 3 * FF] = b[way * rows_z : (way + 1) * rows_z]
 
     def rs_piece(way, s, u):
         rows = slice(u * half, (u + 1) * half)
@@ -548,30 +563,31 @@
     rs_grads(1)
     rs_pieces(1, lambda waits: not waits)
 
+    for q in range(Q):
+        n = nz // Q
+        w_q = w_all[q * n : (q + 1) * n, :, 2 * FF : 3 * FF].reshape(DQ, FF)
+        got = dot(hid[...], w_q, 1, 1).astype(BF16)
+        for g in range(groups):
+            eo[g, q * GX : (q + 1) * GX, :] = got[g * GX : (g + 1) * GX, :]
     for g in range(groups):
-        h_g = hid[g * GX : (g + 1) * GX, :]
-        parts = []
-        for q in range(Q):
-            n = nz // Q
-            w_q = w_all[q * n : (q + 1) * n, :, 2 * FF : 3 * FF].reshape(DQ, FF)
-            parts.append(dot(h_g, w_q, 1, 1).astype(BF16))
-        stacked = jnp.concatenate(parts, axis=0)
-        r_send[pl.ds(g * GR, GR)] = dot(perm, stacked, 0, 0).astype(BF16).reshape(GR, RB, DQ)
+        r_send[pl.ds(g * GR, GR)] = dot(perm, eo[g], 0, 0).astype(BF16).reshape(GR, RB, DQ)
         send_group(g, r_send, r_recv, r_ss, r_rs, -1)
     r_recv[0] = r_send[0]
 
     rs_pieces(1, lambda waits: waits)
+    first_mix = min(5, steps)
 
     for s in range(2, steps + 1):
         if s < steps:
             rs_grads(s)
             rs_pieces(s, always)
-        if s == (5 if steps > 5 else steps):
+        if s == first_mix:
             for g in range(groups):
                 wait_bytes(group_ref(g, r_recv), r_rs.at[g])
-            back = r_recv[...].reshape(ns * RB, DQ)
-            for q in range(Q):
+        for q in range(Q):
+            if s == min(first_mix + q, steps):
                 cols = slice(q * DQ, (q + 1) * DQ)
+                back = r_recv[...].reshape(ns * RB, DQ)
                 got = dot(placeg[q * T : (q + 1) * T, :], back)
                 mixed_ref[0, :, cols] = (stream[:, cols] + got).astype(BF16)
 
@@ -603,6 +619,16 @@
     wait_bytes(x_send.at[pl.ds(1, ns - 1)], x_ss)
     wait_bytes(g_send.at[pl.ds(1, ns - 1)], g_sem.at[0])
     wait_bytes(r_send.at[pl.ds(1, ns - 1)], r_ss)
+
+
+def leave(*refs):
+    n = len(refs) // 2
+    sems = refs[-1]
+    copies = [pltpu.make_async_copy(refs[i], refs[n + i], sems.at[i]) for i in range(n)]
+    for c in copies:
+        c.start()
+    for c in copies:
+        c.wait()
 
 
 def body(
@@ -652,7 +678,6 @@
         vm((chips, PR, HD), BF16),
         vm((chips, PR, HD), BF16),
         vm((nc, chips, PR, HD), BF16),
-        vm((H, T, T), BF16),
         vm((T, D), F32),
         vm((Q * T, DQ), BF16),
         vm((groups, GR * RB, Q * T), BF16),
@@ -672,6 +697,7 @@
         vm((R, FF), BF16),
         vm((ns, RB, DQ), BF16),
         vm((ns, RB, DQ), BF16),
+        vm((groups, GR * RB, DQ), BF16),
         vm((2, rows_z, 3 * FF), F32),
         vm((2, steps, rows_z, 3 * FF), BF16),
         vm((2, steps, rows_z, 3 * FF), BF16),
@@ -690,7 +716,7 @@
     ]
     anywhere = pl.BlockSpec(memory_space=pl.ANY)
     in_vmem = pl.BlockSpec(memory_space=pltpu.VMEM)
-    return pl.pallas_call(
+    outs = pl.pallas_call(
         functools.partial(kernel, grid3, slots),
         out_shape=(
             pltpu.VMEM((1, T, D), BF16),
@@ -723,6 +749,14 @@
         w_down,
         trainable,
     )
+    return pl.pallas_call(
+        leave,
+        out_shape=tuple(jax.ShapeDtypeStruct(o.shape, o.dtype) for o in outs),
+        in_specs=[in_vmem] * len(outs),
+        out_specs=(anywhere,) * len(outs),
+        scratch_shapes=[dma((len(outs),))],
+        name="leave",
+    )(*(pltpu.with_memory_space_constraint(o, pltpu.VMEM) for o in outs))
 
 
 def solution(mesh, grid3=(4, 4, 2)):

time: 113 us -> 111 us (0.982)
  the two profiles are of different devices: /device:TPU:26 before, /device:TPU:2 now
where the time goes in v3:
time: 111 us
  Pallas kernels  109 us (98%)
  between operations  1.45 us (1%)
    pallas_call x1, Pallas kernels, body(): pl.pallas_call(functools.partial(kernel, grid3, slots), out_shape=(pltpu....  108 us

profile of v3, /device:TPU:2, one launch (start us, length us, event | category | flops | bytes accessed | tf_op | source)
XLA Modules:
  0.0 110.6 jit_solution(14015857314049116723)
XLA Ops:
  1.3 108.2 %layer.1 = (bf16[1,128,2048]{2,1,0:T(8,128)(2,1)S(1)}, f32[1,128,256]{2,1,0:T(8,128)S(1)}, f32[1,128,256]{2,1,0:T(8,128)S(1)}, f32[1,128,256]{2,1,0:T(8,128)S(1)}) custom-call(bf16[1,128,2048]{2,1,0:T(8,128)(2,1)} %q_in.1, bf16[1,128,2048]{2,1,0:T(8,128)(2,1)} %k_in.1, bf16[1,128,2048]{2,1,0:T(8,128)(2,1)} %v_in.1, bf16[1,128,2048]{2,1,0:T(8,128)(2,1)} %res_in.1, ...), custom_call_target="tpu_custom_call" | custom-call | tf_op jit(solution)/shard_map/layer/pallas_call | solution.py:719
  109.5 1.0 leave.1

commit v4 on v3

--- a/solution.py
+++ b/solution.py
@@ -306,17 +306,6 @@
     )
     g_send[...] = g_msg.astype(BF16).reshape(ns, 16, 128)
 
-    loads["q"].wait()
-    causal = lax.broadcasted_iota(jnp.int32, (T, T), 0) >= lax.broadcasted_iota(
-        jnp.int32, (T, T), 1
-    )
-    for h in range(H):
-        sl = slice(h * HD, (h + 1) * HD)
-        scores = dot(q_ref[:, sl], k_ref[:, sl], 1, 1)
-        weights = jnp.where(causal, scores, 0.0).astype(BF16)
-        stream[:, sl] = dot(weights, v_ref[:, sl])
-    loads["res"].wait()
-
     pl.semaphore_wait(barrier, ns - 1 + 2)
     pump_to(0)
 
@@ -350,6 +339,17 @@
                 device_id={"seq": to},
                 device_id_type=MESH,
             ).start()
+
+    loads["q"].wait()
+    causal = lax.broadcasted_iota(jnp.int32, (T, T), 0) >= lax.broadcasted_iota(
+        jnp.int32, (T, T), 1
+    )
+    for h in range(H):
+        sl = slice(h * HD, (h + 1) * HD)
+        scores = dot(q_ref[:, sl], k_ref[:, sl], 1, 1)
+        weights = jnp.where(causal, scores, 0.0).astype(BF16)
+        stream[:, sl] = dot(weights, v_ref[:, sl])
+    loads["res"].wait()
 
     pair_a.wait_recv()
     cs_send[...] = (st[mc].astype(F32) + sib[...].astype(F32)).astype(BF16)

time: 111 us -> 108 us (0.973)
  Pallas kernels: 109 us -> 107 us
    pallas_call x1, Pallas kernels: 108 us -> 106 us  [body(): pl.pallas_call(functools.partial(kernel, grid3, slots), out_shape=(pltpu....]
where the time goes in v4:
time: 108 us
  Pallas kernels  107 us (99%)
  between operations  1.45 us (1%)
    pallas_call x1, Pallas kernels, body(): pl.pallas_call(functools.partial(kernel, grid3, slots), out_shape=(pltpu....  106 us

profile of v4, /device:TPU:2, one launch (start us, length us, event | category | flops | bytes accessed | tf_op | source)
XLA Modules:
  0.0 108.3 jit_solution(7140842234606832190)
XLA Ops:
  1.3 105.9 %layer.1 = (bf16[1,128,2048]{2,1,0:T(8,128)(2,1)S(1)}, f32[1,128,256]{2,1,0:T(8,128)S(1)}, f32[1,128,256]{2,1,0:T(8,128)S(1)}, f32[1,128,256]{2,1,0:T(8,128)S(1)}) custom-call(bf16[1,128,2048]{2,1,0:T(8,128)(2,1)} %q_in.1, bf16[1,128,2048]{2,1,0:T(8,128)(2,1)} %k_in.1, bf16[1,128,2048]{2,1,0:T(8,128)(2,1)} %v_in.1, bf16[1,128,2048]{2,1,0:T(8,128)(2,1)} %res_in.1, ...), custom_call_target="tpu_custom_call" | custom-call | tf_op jit(solution)/shard_map/layer/pallas_call | solution.py:719
  107.1 1.0 leave.1
